TPU v7x, 32 devices: a whole 2x2x4 slice. The times are simulated.
32 devices in a mesh: dp: 4 (over y, x), fsdp: 8 (over z, core).
Axes of the slice: x: 2, y: 2, z: 4, core: 2. Of those that a mesh axis runs over, the one named last changes fastest.
Arguments:
- patches: bfloat16 [1536, 6144], P('dp', 'fsdp'), may hold values from -6 to 6
- gain: float32 [6144], replicated, may hold values from 0.1 to 1.9
- w_up: bfloat16 [6144, 12288], P(None, 'fsdp'), may hold values from -0.109375 to 0.109375
- bias: float32 [12288], P('fsdp'), may hold values from -3 to 3
- grad_hidden: bfloat16 [512, 12288], P('dp', 'fsdp'), may hold values from -6 to 6
- patch_counts: int32 [4, 8], replicated, may hold values from 1 to 48, 128 in all within a row
- image_source: int32 [32], replicated, may hold values from 0 to 31, each once
Outputs:
- hidden: bfloat16 [512, 12288], P('dp', 'fsdp')
- grad_patches: bfloat16 [1536, 6144], P('dp', 'fsdp')
- grad_weight: bfloat16 [6144, 12288], P('dp', 'fsdp')
- grad_bias: float32 [12288], P('fsdp')
- gain_gradient: float32 [6144], P('fsdp')
Inputs may be any that keep to these rules, and one draw needn't show every extreme that they name: Each row of patch_counts sums to exactly 128 and has largest entry exactly 48. `image_source`: A permutation: each image number g * 8 + k appears in exactly one slot.
All inputs are finite; a program needn't handle non-finite values.
Results may differ from a plain program's by a relative error of at most 0.0069.
Values may be sent and summed in bfloat16 or wider, within the bound.
A program may use at most 128 MiB of HBM per device.

v0:
```python
import jax
import jax.numpy as jnp
from jax import lax
from jax.sharding import PartitionSpec as P

EPS = 1e-06
ROOT_HALF = 0.7071067811865476
INV_ROOT_TAU = 0.3989422804014327


def gelu_parts(preact):
    normal_cdf = 0.5 * (1.0 + lax.erf(preact * ROOT_HALF))
    density = jnp.exp(-0.5 * preact * preact) * INV_ROOT_TAU
    return (preact * normal_cdf, normal_cdf + preact * density)


def layout(patch_counts, image_source, group_rows, capacity):
    groups, images = patch_counts.shape
    total_images = groups * images
    lengths = patch_counts.reshape(total_images)
    end_rows = jnp.cumsum(patch_counts, axis=1)
    starts = (end_rows - patch_counts).reshape(total_images)
    numbers = jnp.arange(total_images, dtype=jnp.int32)
    slot_of = jnp.sum(
        jnp.where(image_source[None, :] == numbers[:, None], numbers[None, :], 0), axis=1
    )
    row_ids = jnp.arange(group_rows, dtype=jnp.int32)
    position = jnp.sum((row_ids[None, :, None] >= end_rows[:, None, :]).astype(jnp.int32), axis=2)
    image_ids = jnp.arange(groups, dtype=jnp.int32)[:, None] * images + position
    slot_ids = slot_of[image_ids]
    source_row = slot_ids * capacity + row_ids[None, :] - starts[image_ids]
    return (lengths, starts, slot_ids, source_row)


def shards(patches, gain, w_up, bias, grad_hidden, patch_counts, image_source):
    groups = lax.axis_size("dp")
    group_index = lax.axis_index("dp")
    images = patch_counts.shape[1]
    group_rows = grad_hidden.shape[0]
    capacity = patches.shape[0] // images
    local_width = patches.shape[1]
    lengths, starts, slot_ids, source_row = layout(patch_counts, image_source, group_rows, capacity)
    owner = slot_ids // images
    local_row = source_row - owner * (images * capacity)
    picked = patches[local_row.reshape(-1)].reshape(groups, group_rows, local_width)
    is_mine = owner == group_index
    outgoing = jnp.where(is_mine[:, :, None], picked, jnp.zeros_like(picked))
    arrived = lax.all_to_all(outgoing, "dp", split_axis=0, concat_axis=0, tiled=True)
    packed = jnp.sum(arrived.astype(jnp.float32), axis=0).astype(jnp.bfloat16)
    gathered = lax.all_gather(packed, "fsdp", axis=1, tiled=True)
    full_width = gathered.shape[1]
    values = gathered.astype(jnp.float32)
    row_mean = jnp.mean(values, axis=1, keepdims=True)
    centred_input = values - row_mean
    variance = jnp.mean(centred_input * centred_input, axis=1)
    inverse_deviation = lax.rsqrt(variance + EPS)
    normalized_input = centred_input * inverse_deviation[:, None]
    normed_input = (normalized_input * gain).astype(jnp.bfloat16)
    preact = jnp.dot(normed_input, w_up, preferred_element_type=jnp.float32) + bias
    gelu_value, gelu_slope = gelu_parts(preact)
    hidden = gelu_value.astype(jnp.bfloat16)
    feature_gradient = grad_hidden.astype(jnp.float32) * gelu_slope
    grad_pre = feature_gradient.astype(jnp.bfloat16)
    normed_gradient = lax.psum_scatter(
        lax.dot_general(
            w_up, grad_pre, (((1,), (1,)), ((), ())), preferred_element_type=jnp.float32
        ),
        "fsdp",
        scatter_dimension=0,
        tiled=True,
    )
    feature_offset = lax.axis_index("fsdp") * local_width
    normalized_local = lax.dynamic_slice_in_dim(normalized_input, feature_offset, local_width, 1).T
    gain_mine = lax.dynamic_slice_in_dim(gain, feature_offset, local_width, 0)
    scaled_input = gain_mine[:, None] * normed_gradient
    plain_sum, weighted_row_sum = lax.psum(
        (jnp.sum(scaled_input, axis=0), jnp.sum(scaled_input * normalized_local, axis=0)), "fsdp"
    )
    packed_gradient = (
        inverse_deviation[None, :]
        * (
            scaled_input
            - plain_sum[None, :] / full_width
            - normalized_local * weighted_row_sum[None, :] / full_width
        )
    ).T.astype(jnp.bfloat16)
    owned_rows = w_up.shape[0] // groups
    column_rows = lax.all_to_all(normed_input, "dp", split_axis=1, concat_axis=0, tiled=True)
    piece = lax.all_gather(grad_pre, "dp", axis=0, tiled=True)
    blocks = piece.shape[0] // group_rows
    terms = jnp.einsum(
        "gtd,gtf->gdf",
        column_rows.reshape(blocks, group_rows, owned_rows),
        piece.reshape(blocks, group_rows, piece.shape[1]),
        preferred_element_type=jnp.float32,
    )
    rounded = lax.optimization_barrier(terms.astype(jnp.bfloat16)).astype(jnp.float32)
    grad_weight = jnp.sum(rounded, axis=0).astype(jnp.bfloat16)
    gain_gradient, grad_bias = lax.psum(
        (jnp.sum(normed_gradient * normalized_local, axis=1), jnp.sum(feature_gradient, axis=0)),
        "dp",
    )
    offsets = jnp.arange(capacity, dtype=jnp.int32)
    all_images = image_source.reshape(groups, images)
    target = all_images // images
    counts = lengths[all_images]
    usable = (target == group_index)[:, :, None] & (offsets[None, None, :] < counts[:, :, None])
    rows_at = jnp.minimum(starts[all_images][:, :, None] + offsets[None, None, :], group_rows - 1)
    pieces = packed_gradient[rows_at.reshape(-1)].reshape(groups, images * capacity, local_width)
    outgoing_back = jnp.where(
        usable.reshape(groups, images * capacity)[:, :, None], pieces, jnp.zeros_like(pieces)
    )
    returned = lax.all_to_all(outgoing_back, "dp", split_axis=0, concat_axis=0, tiled=True)
    grad_patches = jnp.sum(returned.astype(jnp.float32), axis=0).astype(jnp.bfloat16)
    return (hidden, grad_patches, grad_weight, grad_bias, gain_gradient)


def solution(mesh):
    return jax.shard_map(
        shards,
        mesh=mesh,
        in_specs=(P("dp", "fsdp"), P(), P(None, "fsdp"), P("fsdp"), P("dp", "fsdp"), P(), P()),
        out_specs=(P("dp", "fsdp"), P("dp", "fsdp"), P("dp", "fsdp"), P("fsdp"), P("fsdp")),
        check_vma=False,
    )
```

profile of v0, /device:TPU:0, one launch (start us, length us, event | category | flops | bytes accessed | tf_op | source)
XLA Modules:
  0.0 225.8 jit_solution(12741459276163575788)
XLA Ops:
  7.2 0.9 reduce_window_sum.11
  8.2 0.7 sub.59
  8.8 0.1 convert_reduce_fusion.1
  8.9 0.8 select_reduce_fusion
  9.7 0.1 reshape.348
  9.8 0.1 fusion.21
  9.9 3.3 %gather_fusion = s32[512]{0:T(512)S(1)} fusion(s32[32]{0:T(128)S(1)} %select_reduce_fusion, s32[1024]{0:T(1024)S(1)} %pad_clamp_fusion.3), kind=kCustom, calls=%fused_computation | custom fusion | bytes 6144 | tf_op jit(solution)/shard_map/gather | solution.py:30
  13.2 3.3 %gather_fusion.1 = s32[512]{0:T(512)S(1)} fusion(s32[32]{0:T(128)S(1)} %reshape.348, s32[1024]{0:T(1024)S(1)} %pad_clamp_fusion.3), kind=kCustom, calls=%fused_computation.1 | custom fusion | bytes 6144 | tf_op jit(solution)/shard_map/gather | solution.py:31
  16.6 2.0 gather_fusion.2
  18.7 0.1 broadcast_select_fusion.1
  18.8 16.3 %all_to_all.26 = bf16[4,128,768]{2,1,0:T(8,128)(2,1)S(1)} all-to-all(bf16[4,128,768]{2,1,0:T(8,128)(2,1)S(1)} %broadcast_select_fusion.1), channel_id=1, replica_groups=mesh['dp'=4,'fsdp'=8] {'dp'}, dimensions={0} | all-to-all | bytes 1572864 | tf_op jit(solution)/shard_map/all_to_all | solution.py:48
  35.1 0.8 reduce_sum.113
  36.0 24.9 %all-gather.3.cloned.1.call-done = bf16[128,6144]{1,0:T(8,128)(2,1)} async-done(((bf16[128,768]{1,0:T(8,128)(2,1)}), bf16[128,6144]{1,0:T(8,128)(2,1)}) %all-gather.3.cloned.1.call-update) | async-done | bytes 1572880 | tf_op jit(solution)/shard_map/all_gather | solution.py:50
  60.9 1.8 convert_reduce_fusion
  62.7 2.0 fusion.2
  64.8 2.3 %fusion = (f32[128,6144]{1,0:T(8,128)}, bf16[128,6144]{1,0:T(8,128)(2,1)S(1)}) fusion(bf16[128,6144]{1,0:T(8,128)(2,1)S(1)} %copy-done.2, f32[128]{0:T(128)S(1)} %add_rsqrt_fusion, f32[128]{0:T(128)S(1)} %broadcast_multiply_fusion.1, f32[6144]{0:T(1024)S(1)} %copy-done.5), kind=kLoop, calls=%fused_computation.10 | loop fusion | flops 3932160 | bytes 6317056 | tf_op jit(solution)/shard_map/mul | solution.py:57
  67.1 10.2 %fusion.25 = (f32[1536]{0:T(1024)S(1)}, bf16[128,1536]{1,0:T(8,128)(2,1)S(1)}, bf16[128,1536]{1,0:T(8,128)(2,1)}) fusion(bf16[128,1536]{1,0:T(8,128)(2,1)S(1)} %copy-done.4, f32[1536]{0:T(1024)S(1)} %copy-done.7, bf16[128,6144]{1,0:T(8,128)(2,1)S(1)} %get-tuple-element.13, bf16[6144,1536]{1,0:T(8,128)(2,1)} %param.9), kind=kOutput, calls=%fused_computation.80 | convolution fusion | flops 2418866688 | bytes 21639168 | tf_op jit(solution)/shard_map/dot_general | solution.py:59
  77.2 14.3 %convolution_bitcast_fusion = f32[6144,128]{0,1:T(8,128)} fusion(bf16[128,1536]{1,0:T(8,128)(2,1)S(1)} %get-tuple-element.15, bf16[6144,1536]{1,0:T(8,128)(2,1)} %param.9), kind=kOutput, calls=%fused_computation.7 | convolution fusion | flops 2415919104 | bytes 22413312 | tf_op jit(solution)/shard_map/dot_general | solution.py:65
  91.6 0.6 copy-done.8
  92.2 0.1 reshape.352
  92.3 0.1 reshape.350
  92.3 0.1 reshape.381
  92.4 0.7 gather_fusion.4
  93.1 0.1 reshape.388
  93.2 0.1 add_minimum_fusion
  93.3 0.1 min.19
  93.5 1.6 copy.15
  95.1 4.3 %all-to-all-start.2 = ((bf16[128,4,1536]{0,2,1:T(8,128)(2,1)}), bf16[128,4,1536]{0,2,1:T(8,128)(2,1)}, u32[]{:S(2)}, u32[]{:S(2)}) async-start(bf16[128,4,1536]{0,2,1:T(8,128)(2,1)} %bitcast.63), calls=%async_computation.3 | async-start | bytes 3145728 | tf_op jit(solution)/shard_map/all_to_all | solution.py:88
  99.4 0.1 reshape.351
  99.5 0.7 gather_fusion.3
  100.2 0.1 reshape.380
  100.3 0.1 and.63
  100.4 0.1 and.64
  100.5 0.1 dynamic_slice.6
  100.6 0.1 lt.70
  100.7 0.1 lt.73
  100.8 30.7 %reduce-scatter.2.cloned.1.call-done = f32[768,128]{0,1:T(8,128)} async-done(((f32[6144,128]{0,1:T(8,128)}), f32[768,128]{0,1:T(8,128)}) %reduce-scatter.2.cloned.1.call-update) | async-done | bytes 393232 | tf_op jit(solution)/shard_map/reduce_scatter | solution.py:64
  131.5 1.3 fusion.14
  132.8 15.1 %all-reduce = (f32[128]{0:T(128)S(1)}, f32[128]{0:T(128)S(1)}) all-reduce(f32[128]{0:T(128)S(1)} %get-tuple-element.6, f32[128]{0:T(128)S(1)} %get-tuple-element.7), channel_id=1, replica_groups=mesh['dp'=4,'fsdp'=8] {'fsdp'}, use_global_device_ids=true, to_apply=%region_10.11 | all-reduce | flops 256 | bytes 2048 | tf_op jit(solution)/shard_map/psum | solution.py:76
  147.9 1.3 fusion.15
  149.2 5.0 %gather_fusion.5 = bf16[1536,768]{1,0:T(8,128)(2,1)S(1)} fusion(bf16[128,768]{1,0:T(8,128)(2,1)S(1)} %fusion.15, s32[2048]{0:T(1024)S(1)} %pad_clamp_fusion), kind=kCustom, calls=%fused_computation.5 | custom fusion | bytes 4724736 | tf_op jit(solution)/shard_map/gather | solution.py:109
  154.2 1.7 broadcast_select_fusion
  155.9 3.8 %all-to-all-start.1 = ((bf16[4,384,768]{2,1,0:T(8,128)(2,1)}), bf16[4,384,768]{2,1,0:T(8,128)(2,1)S(1)}, u32[]{:S(2)}, u32[]{:S(2)}) async-start(bf16[4,384,768]{2,1,0:T(8,128)(2,1)} %broadcast_select_fusion), calls=%async_computation.2 | async-start | bytes 4718592 | tf_op jit(solution)/shard_map/all_to_all | solution.py:113
  159.7 19.6 %all-gather.5.cloned.1.call-done = bf16[512,1536]{1,0:T(8,128)(2,1)} async-done(((bf16[128,1536]{1,0:T(8,128)(2,1)}), bf16[512,1536]{1,0:T(8,128)(2,1)}) %all-gather.5.cloned.1.call-update) | async-done | bytes 1572880 | tf_op jit(solution)/shard_map/all_gather | solution.py:89
  179.3 10.8 %convolution_convert_fusion = bf16[4,1536,1536]{2,1,0:T(8,128)(2,1)} fusion(bf16[4,128,1536]{2,1,0:T(8,128)(2,1)} %bitcast.65, bf16[128,4,1536]{0,2,1:T(8,128)(2,1)} %all-to-all-done.2), kind=kOutput, calls=%fused_computation.6 | convolution fusion | flops 2425356288 | bytes 22020096 | tf_op jit(solution)/shard_map/gtd,gtf->gdf/dot_general | solution.py:91
  190.1 13.5 %reduce_sum.119 = bf16[1536,1536]{1,0:T(8,128)(2,1)} reduce(bf16[4,1536,1536]{2,1,0:T(8,128)(2,1)} %convolution_convert_fusion, bf16[]{:T(256)} %constant.74.clone.1), dimensions={0}, to_apply=%region_12.13 | reduce | flops 7077888 | bytes 23592962 | tf_op jit(solution)/shard_map/reduce_sum | solution.py:98
  203.6 14.3 %all-reduce.1 = (f32[1536]{0:T(1024)}, f32[768]{0:T(1024)}) all-reduce(f32[1536]{0:T(1024)S(1)} %get-tuple-element.14, f32[768]{0:T(1024)S(1)} %get-tuple-element.5), channel_id=1, replica_groups=mesh['dp'=4,'fsdp'=8] {'dp'}, use_global_device_ids=true, to_apply=%region_14.15 | all-reduce | flops 2304 | bytes 18432 | tf_op jit(solution)/shard_map/psum | solution.py:99
  218.0 1.3 reduce_sum.118
  (42 shorter events, 0.4 us)
Async XLA Ops:
  7.2 9.5 %copy-start = (bf16[384,768]{1,0:T(8,128)(2,1)S(1)}, bf16[384,768]{1,0:T(8,128)(2,1)}, u32[]{:S(2)}) copy-start(bf16[384,768]{1,0:T(8,128)(2,1)} %param.7) | copy-start | bytes 1769476
  7.2 53.7 %all-gather.3.cloned.1.call-start = ((), (), s32[]{:S(2)}) async-start(), calls=%async_computation.4 | async-start | bytes 1769472 | tf_op jit(solution)/shard_map/all_gather | solution.py:50
  18.8 45.9 %copy-start.5 = (f32[6144]{0:T(1024)S(1)}, f32[6144]{0:T(1024)}, u32[]{:S(2)}) copy-start(f32[6144]{0:T(1024)} %param.8) | copy-start | bytes 73732
  36.0 95.5 %reduce-scatter.2.cloned.1.call-start = ((), (), s32[]{:S(2)}) async-start(), calls=%async_computation.5 | async-start | bytes 3538944 | tf_op jit(solution)/shard_map/reduce_scatter | solution.py:64
  60.9 3.8 %copy-start.2 = (bf16[128,6144]{1,0:T(8,128)(2,1)S(1)}, bf16[128,6144]{1,0:T(8,128)(2,1)}, u32[]{:S(2)}) copy-start(bf16[128,6144]{1,0:T(8,128)(2,1)} %all-gather.3.cloned.1.call-done) | copy-start | bytes 4718596
  64.7 2.3 %copy-start.4 = (bf16[128,1536]{1,0:T(8,128)(2,1)S(1)}, bf16[128,1536]{1,0:T(8,128)(2,1)}, u32[]{:S(2)}) copy-start(bf16[128,1536]{1,0:T(8,128)(2,1)} %param.11) | copy-start | bytes 1179652
  64.8 2.3 %copy-start.7 = (f32[1536]{0:T(1024)S(1)}, f32[1536]{0:T(1024)}, u32[]{:S(2)}) copy-start(f32[1536]{0:T(1024)} %param.10) | copy-start | bytes 18436
  77.2 14.3 %copy-start.3 = (bf16[128,1536]{1,0:T(8,128)(2,1)}, bf16[128,1536]{1,0:T(8,128)(2,1)S(1)}, u32[]{:S(2)}) copy-start(bf16[128,1536]{1,0:T(8,128)(2,1)S(1)} %get-tuple-element.15) | copy-start | bytes 1179652
  91.5 0.7 copy-start.8
  91.5 87.7 %all-gather.5.cloned.1.call-start = ((), (), s32[]{:S(2)}) async-start(), calls=%async_computation.6 | async-start | bytes 1966080 | tf_op jit(solution)/shard_map/all_gather | solution.py:89
  93.5 5.9 %copy-start.6 = (s32[4,8]{1,0:T(4,128)S(1)}, s32[4,8]{1,0:T(4,128)}, u32[]{:S(2)}) copy-start(s32[4,8]{1,0:T(4,128)} %param.12) | copy-start | bytes 388
  95.1 60.8 %all-to-all-start.2 = ((bf16[128,4,1536]{0,2,1:T(8,128)(2,1)}), bf16[128,4,1536]{0,2,1:T(8,128)(2,1)}, u32[]{:S(2)}, u32[]{:S(2)}) async-start(bf16[128,4,1536]{0,2,1:T(8,128)(2,1)} %bitcast.63), calls=%async_computation.3 | async-start | bytes 3145728 | tf_op jit(solution)/shard_map/all_to_all | solution.py:88
  155.9 62.1 %all-to-all-start.1 = ((bf16[4,384,768]{2,1,0:T(8,128)(2,1)}), bf16[4,384,768]{2,1,0:T(8,128)(2,1)S(1)}, u32[]{:S(2)}, u32[]{:S(2)}) async-start(bf16[4,384,768]{2,1,0:T(8,128)(2,1)} %broadcast_select_fusion), calls=%async_computation.2 | async-start | bytes 4718592 | tf_op jit(solution)/shard_map/all_to_all | solution.py:113
  190.1 29.2 %copy-start.1 = (bf16[384,768]{1,0:T(8,128)(2,1)S(1)}, bf16[384,768]{1,0:T(8,128)(2,1)}, u32[]{:S(2)}) copy-start(bf16[384,768]{1,0:T(8,128)(2,1)} %param.7) | copy-start | bytes 1769476
Sparse Core Ops, SparseCore 0:
  36.1 24.7 all-gather.2
  91.7 39.7 reduce-scatter.1
  133.9 45.2 all-gather.4
where the time goes:
time: 230 us; the launch traced here: 226 us
  waiting for transfers between devices  75.2 us (33%)
  blocking collectives  45.8 us (20%)
  matrix products  35.2 us (15%)
  other arithmetic  28.9 us (13%)
  local copies, waits for them, and re-layouts  18.5 us (8%)
  between operations  14 us (6%)
  starting transfers between devices  8.28 us (4%)
    reduce_scatter x1, waiting for transfers between devices, shards(): lax.psum_scatter(lax.dot_general(w_up, grad_pre, (((1,), (1,)), ((), ()))...  30.7 us
    all_gather x1, waiting for transfers between devices, shards(): gathered = lax.all_gather(packed, 'fsdp', axis=1, tiled=True)  24.9 us
    all_gather x1, waiting for transfers between devices, shards(): piece = lax.all_gather(grad_pre, 'dp', axis=0, tiled=True)  19.6 us
    all_to_all x1, blocking collectives, shards(): lax.all_to_all(outgoing, 'dp', split_axis=0, concat_axis=0, tiled=True)  16.3 us
    psum x1, blocking collectives, shards(): lax.psum((jnp.sum(scaled_input, axis=0), jnp.sum(scaled_input * normalize...  15.1 us
    psum x1, blocking collectives, shards(): lax.psum((jnp.sum(normed_gradient * normalized_local, axis=1), jnp.sum(fe...  14.3 us
    dot_general x1, matrix products, shards(): lax.dot_general(w_up, grad_pre, (((1,), (1,)), ((), ())), preferred_eleme...  14.3 us
    reduce_sum x1, other arithmetic, shards(): grad_weight = jnp.sum(rounded, axis=0).astype(jnp.bfloat16)  13.5 us
  transfers between devices with their start and end apart: 5, of which 3 were waited for; matrix products, arithmetic and copies ran while one was open for 17% of the time, Pallas kernels for 0%

commit v1 on v0

v1 whole, which is shorter than its diff:
```python
import jax
import jax.numpy as jnp
from jax import lax
from jax.sharding import PartitionSpec as P

EPS = 1e-06
ROOT_HALF = 0.7071067811865476
INV_ROOT_TAU = 0.3989422804014327


def gelu_parts(preact):
    normal_cdf = 0.5 * (1.0 + lax.erf(preact * ROOT_HALF))
    density = jnp.exp(-0.5 * preact * preact) * INV_ROOT_TAU
    return (preact * normal_cdf, normal_cdf + preact * density)


def destination_rows(patch_counts, image_source, group_index, group_rows, capacity):
    groups, images = patch_counts.shape
    total_images = groups * images
    starts = (jnp.cumsum(patch_counts, axis=1) - patch_counts).reshape(total_images)
    lengths = patch_counts.reshape(total_images)
    mine = lax.dynamic_slice_in_dim(image_source, group_index * images, images, 0)
    chosen = mine[:, None] == jnp.arange(total_images, dtype=jnp.int32)[None, :]
    start = jnp.sum(jnp.where(chosen, starts[None, :], 0), axis=1)
    count = jnp.sum(jnp.where(chosen, lengths[None, :], 0), axis=1)
    offsets = jnp.arange(capacity, dtype=jnp.int32)
    first = (mine // images) * group_rows + start
    rows = jnp.where(offsets[None, :] < count[:, None], first[:, None] + offsets[None, :], -1)
    return rows.reshape(images * capacity)


def split_in_two(values):
    high = values.astype(jnp.bfloat16)
    low = (values - high.astype(jnp.float32)).astype(jnp.bfloat16)
    return high, low


def middle(outgoing, gain, w_up, bias, grad_hidden):
    groups, group_rows, local_width = outgoing.shape
    shards_of = lax.axis_size("fsdp")
    arrived = lax.all_to_all(outgoing, "dp", split_axis=0, concat_axis=0, tiled=True)
    packed = jnp.sum(arrived.astype(jnp.float32), axis=0).astype(jnp.bfloat16)
    gathered = lax.all_gather(packed, "fsdp", axis=1, tiled=True)
    full_width = gathered.shape[1]
    values = gathered.astype(jnp.float32)
    row_mean = jnp.mean(values, axis=1, keepdims=True)
    centred_input = values - row_mean
    variance = jnp.mean(centred_input * centred_input, axis=1)
    inverse_deviation = lax.rsqrt(variance + EPS)
    normalized_input = centred_input * inverse_deviation[:, None]
    normed_input = (normalized_input * gain).astype(jnp.bfloat16)
    preact = jnp.dot(normed_input, w_up, preferred_element_type=jnp.float32) + bias
    gelu_value, gelu_slope = gelu_parts(preact)
    hidden = gelu_value.astype(jnp.bfloat16)
    feature_gradient = grad_hidden.astype(jnp.float32) * gelu_slope
    grad_pre = feature_gradient.astype(jnp.bfloat16)
    piece = lax.all_gather(grad_pre, "dp", axis=0, tiled=True)
    column_rows = lax.all_to_all(normed_input, "dp", split_axis=1, concat_axis=0, tiled=True)
    partial = lax.dot_general(
        w_up, grad_pre, (((1,), (1,)), ((), ())), preferred_element_type=jnp.float32
    )
    scaled_partial = partial * gain[:, None]
    sums = jnp.stack(
        [jnp.sum(scaled_partial, axis=0), jnp.sum(scaled_partial * normalized_input.T, axis=0)]
    )
    high, low = split_in_two(sums)
    extra = jnp.concatenate([high, low, jnp.zeros((12, group_rows), jnp.bfloat16)])
    sent = jnp.concatenate(
        [
            partial.astype(jnp.bfloat16).reshape(shards_of, local_width, group_rows),
            jnp.broadcast_to(extra[None], (shards_of,) + extra.shape),
        ],
        axis=1,
    )
    parts = lax.all_to_all(sent, "fsdp", split_axis=0, concat_axis=0, tiled=True)
    total = jnp.sum(parts.astype(jnp.float32), axis=0)
    normed_gradient = total[:local_width]
    row_sums = total[local_width : local_width + 2] + total[local_width + 2 : local_width + 4]
    feature_offset = lax.axis_index("fsdp") * local_width
    own_input = lax.dynamic_slice_in_dim(gathered, feature_offset, local_width, 1)
    normalized_local = (
        (own_input.astype(jnp.float32) - row_mean) * inverse_deviation[:, None]
    ).T
    gain_mine = lax.dynamic_slice_in_dim(gain, feature_offset, local_width, 0)
    packed_gradient = (
        inverse_deviation[None, :]
        * (
            gain_mine[:, None] * normed_gradient
            - row_sums[0][None, :] / full_width
            - normalized_local * row_sums[1][None, :] / full_width
        )
    ).T.astype(jnp.bfloat16)
    high, low = split_in_two(jnp.sum(normed_gradient * normalized_local, axis=1))
    back = jnp.concatenate(
        [packed_gradient, high[None], low[None], jnp.zeros((14, local_width), jnp.bfloat16)]
    )
    all_back = lax.all_gather(back, "dp", axis=0)
    gain_gradient = jnp.sum(
        all_back[:, group_rows : group_rows + 2].astype(jnp.float32), axis=(0, 1)
    )
    gradients = all_back[:, :group_rows].reshape(groups * group_rows, local_width)
    return hidden, column_rows, piece, gradients, gain_gradient


def shards(patches, gain, w_up, bias, grad_hidden, patch_counts, image_source):
    groups, images = patch_counts.shape
    group_rows = grad_hidden.shape[0]
    capacity = patches.shape[0] // images
    local_width = patches.shape[1]
    rows = destination_rows(
        patch_counts, image_source, lax.axis_index("dp"), group_rows, capacity
    )
    numbers = jnp.arange(groups * group_rows, dtype=jnp.int32)
    placed = (rows[None, :] == numbers[:, None]).astype(jnp.bfloat16)
    outgoing = jnp.dot(placed, patches, preferred_element_type=jnp.float32)
    outgoing = outgoing.astype(jnp.bfloat16).reshape(groups, group_rows, local_width)
    hidden, column_rows, piece, gradients, gain_gradient = middle(
        outgoing, gain, w_up, bias, grad_hidden
    )
    grad_weight = lax.dot_general(
        column_rows, piece, (((0,), (0,)), ((), ())), preferred_element_type=jnp.float32
    ).astype(jnp.bfloat16)
    grad_bias = jnp.sum(piece.astype(jnp.float32), axis=0)
    grad_patches = lax.dot_general(
        placed, gradients, (((0,), (0,)), ((), ())), preferred_element_type=jnp.float32
    ).astype(jnp.bfloat16)
    return (hidden, grad_patches, grad_weight, grad_bias, gain_gradient)


def solution(mesh):
    return jax.shard_map(
        shards,
        mesh=mesh,
        in_specs=(P("dp", "fsdp"), P(), P(None, "fsdp"), P("fsdp"), P("dp", "fsdp"), P(), P()),
        out_specs=(P("dp", "fsdp"), P("dp", "fsdp"), P("dp", "fsdp"), P("fsdp"), P("fsdp")),
        check_vma=False,
    )
```

time: 230 us -> 154 us (0.67); the launches traced: 226 us -> 154 us
  waiting for transfers between devices: 75.2 us -> 54.2 us
  blocking collectives: 45.8 us -> 28.4 us
  other arithmetic: 28.9 us -> 13.5 us
  local copies, waits for them, and re-layouts: 18.5 us -> 5.44 us
  matrix products: 35.2 us -> 30 us
    reduce_scatter x1 -> x0, waiting for transfers between devices: 30.7 us -> none  [shards(): lax.psum_scatter(lax.dot_general(w_up, grad_pre, (((1,), (1,)), ((), ()))...]
    psum x2 -> x0, blocking collectives: 29.5 us -> none  [the longest x1 15.1 us: shards(): lax.psum((jnp.sum(scaled_input, axis=0), jnp.sum(scaled_input * normalize...]
    all_to_all x2, waiting for transfers between devices: 0.01 us -> 16.5 us  [the longest x1 16.5 us: middle(): lax.all_to_all(sent, 'fsdp', split_axis=0, concat_axis=0, tiled=True)]
    gather x8 -> x0, local copies, waits for them, and re-layouts: 15.3 us -> none  [the longest x1 4.97 us: shards(): packed_gradient[rows_at.reshape(-1)]]
    reduce_sum x8 -> x7, other arithmetic: 21.6 us -> 7.89 us  [the longest x1 2.26 us: shards(): grad_bias = jnp.sum(piece.astype(jnp.float32), axis=0)]
    all_gather x0 -> x1, blocking collectives: none -> 12.2 us  [middle(): all_back = lax.all_gather(back, 'dp', axis=0)]
    all_gather x2, waiting for transfers between devices: 44.5 us -> 37.7 us  [the longest x1 24.8 us: middle(): gathered = lax.all_gather(packed, 'fsdp', axis=1, tiled=True)]
    dot_general x3 -> x5, matrix products: 35.2 us -> 30 us  [the longest x1 11.2 us: middle(): lax.dot_general(w_up, grad_pre, (((1,), (1,)), ((), ())), preferred_eleme...]
  transfers between devices with their start and end apart: 5 -> 4, of which waited for: 3 -> 3; matrix products, arithmetic and copies ran while one was open for 17% -> 22% of each run, Pallas kernels for 0% -> 0%
where the time goes in v1:
time: 154 us
  waiting for transfers between devices  54.2 us (35%)
  matrix products  30 us (19%)
  blocking collectives  28.4 us (18%)
  between operations  14.3 us (9%)
  other arithmetic  13.5 us (9%)
  starting transfers between devices  8.01 us (5%)
  local copies, waits for them, and re-layouts  5.44 us (4%)
    all_gather x1, waiting for transfers between devices, middle(): gathered = lax.all_gather(packed, 'fsdp', axis=1, tiled=True)  24.8 us
    all_to_all x1, waiting for transfers between devices, middle(): lax.all_to_all(sent, 'fsdp', split_axis=0, concat_axis=0, tiled=True)  16.5 us
    all_to_all x1, blocking collectives, middle(): lax.all_to_all(outgoing, 'dp', split_axis=0, concat_axis=0, tiled=True)  16.3 us
    all_gather x1, waiting for transfers between devices, middle(): piece = lax.all_gather(grad_pre, 'dp', axis=0, tiled=True)  12.8 us
    all_gather x1, blocking collectives, middle(): all_back = lax.all_gather(back, 'dp', axis=0)  12.2 us
    dot_general x1, matrix products, middle(): lax.dot_general(w_up, grad_pre, (((1,), (1,)), ((), ())), preferred_eleme...  11.2 us
    dot_general x1, matrix products, middle(): jnp.dot(normed_input, w_up, preferred_element_type=jnp.float32) + bias  10.2 us
    dot_general x1, matrix products, shards(): lax.dot_general(column_rows, piece, (((0,), (0,)), ((), ())), preferred_e...  6.72 us
  transfers between devices with their start and end apart: 4, of which 3 were waited for; matrix products, arithmetic and copies ran while one was open for 22% of the time, Pallas kernels for 0%

profile of v1, /device:TPU:0, one launch (start us, length us, event | category | flops | bytes accessed | tf_op | source)
XLA Modules:
  0.0 153.8 jit_solution(9181044650758408426)
XLA Ops:
  7.2 0.0 copy-start
  7.2 0.0 all-gather.4.cloned.1.call-start
  7.2 0.8 broadcast_in_dim.32
  8.0 0.9 reduce_window_sum.11
  8.9 0.7 sub.50
  9.6 0.1 broadcast_in_dim.58
  9.7 0.7 dynamic_slice.9
  10.4 0.2 select_reduce_fusion.1
  10.6 0.7 multiply_add_fusion
  11.3 0.1 add_select_fusion
  11.4 0.1 select_n.35
  11.5 0.6 convolution_convert_fusion.1
  12.1 0.0 copy-start.3
  12.1 16.3 %all_to_all.29 = bf16[4,128,768]{2,1,0:T(8,128)(2,1)S(1)} all-to-all(bf16[4,128,768]{2,1,0:T(8,128)(2,1)S(1)} %bitcast.50), channel_id=1, replica_groups=mesh['dp'=4,'fsdp'=8] {'dp'}, dimensions={0} | all-to-all | bytes 1572864 | tf_op jit(solution)/shard_map/all_to_all | solution.py:41
  28.4 0.8 reduce_sum.106
  29.2 0.0 all-gather.4.cloned.1.call-update
  29.2 0.1 pad.8.clone
  29.3 24.8 %all-gather.4.cloned.1.call-done = bf16[128,6144]{1,0:T(8,128)(2,1)} async-done(((bf16[128,768]{1,0:T(8,128)(2,1)}), bf16[128,6144]{1,0:T(8,128)(2,1)}) %all-gather.4.cloned.1.call-update) | async-done | bytes 1572880 | tf_op jit(solution)/shard_map/all_gather | solution.py:43
  54.1 1.8 %convert_reduce_fusion = f32[128]{0:T(128)S(1)} fusion(bf16[128,6144]{1,0:T(8,128)(2,1)} %all-gather.4.cloned.1.call-done), kind=kLoop, calls=%fused_computation.2 | loop fusion | flops 1572736 | bytes 1573376 | tf_op jit(solution)/shard_map/reduce_sum | solution.py:46
  56.0 2.0 %fusion.6 = f32[128]{0:T(128)S(1)} fusion(bf16[128,6144]{1,0:T(8,128)(2,1)} %all-gather.4.cloned.1.call-done, f32[128]{0:T(128)S(1)} %broadcast_multiply_fusion), kind=kLoop, calls=%fused_computation.10 | loop fusion | flops 3145600 | bytes 1573888 | tf_op jit(solution)/shard_map/reduce_sum | solution.py:48
  58.0 0.6 fusion.4
  58.5 0.0 copy-start.2
  58.5 0.0 copy-start.4
  58.6 1.3 copy.29
  59.9 4.3 %all-to-all-start.2 = ((bf16[128,4,1536]{2,0,1:T(8,128)(2,1)}), bf16[128,4,1536]{2,0,1:T(8,128)(2,1)}, u32[]{:S(2)}, u32[]{:S(2)}) async-start(bf16[128,4,1536]{2,0,1:T(8,128)(2,1)} %bitcast.45), calls=%async_computation.2 | async-start | bytes 3145728 | tf_op jit(solution)/shard_map/all_to_all | solution.py:58
  64.2 0.0 all-gather.6.cloned.1.call-start
  64.3 10.2 %fusion.12 = (bf16[128,1536]{1,0:T(8,128)(2,1)}, bf16[128,1536]{1,0:T(8,128)(2,1)}) fusion(bf16[128,1536]{1,0:T(8,128)(2,1)S(1)} %copy-done.2, f32[1536]{0:T(1024)S(1)} %copy-done.4, bf16[128,6144]{1,0:T(8,128)(2,1)S(1)} %fusion.4, bf16[6144,1536]{1,0:T(8,128)(2,1)} %param.9), kind=kOutput, calls=%fused_computation.25 | convolution fusion | flops 2418671616 | bytes 21633024 | tf_op jit(solution)/shard_map/dot_general | solution.py:52
  74.5 0.0 all-gather.6.cloned.1.call-update
  74.5 11.2 %multiply_reduce_fusion = (f32[128]{0:T(128)S(1)}, f32[128]{0:T(128)S(1)}, bf16[6144,128]{0,1:T(8,128)(2,1)}) fusion(f32[6144]{0:T(1024)S(1)} %copy-done.3, f32[128]{0:T(128)S(1)} %add_rsqrt_fusion, f32[128]{0:T(128)S(1)} %broadcast_multiply_fusion, bf16[128,6144]{1,0:T(8,128)(2,1)} %all-gather.4.cloned.1.call-done, ...), kind=kOutput, calls=%fused_computation.12 | convolution fusion | flops 2422210560 | bytes 22439936 | tf_op jit(solution)/shard_map/dot_general | solution.py:59
  85.7 1.9 %copy.25 = bf16[6144,128]{1,0:T(8,128)(2,1)S(1)} copy(bf16[6144,128]{0,1:T(8,128)(2,1)} %get-tuple-element.9) | data formatting | bytes 3145728 | tf_op jit(solution)/shard_map/reshape | solution.py:70
  87.7 0.1 maximum_maximum_fusion.1
  87.8 1.3 pad_maximum_fusion
  89.0 0.0 all-to-all-done.2
  89.0 3.6 %all-to-all-start.1 = ((bf16[8,784,128]{2,1,0:T(8,128)(2,1)}), bf16[8,784,128]{2,1,0:T(8,128)(2,1)S(1)}, u32[]{:S(2)}, u32[]{:S(2)}) async-start(bf16[8,784,128]{2,1,0:T(8,128)(2,1)} %pad_maximum_fusion), calls=%async_computation.1 | async-start | bytes 3211264 | tf_op jit(solution)/shard_map/all_to_all | solution.py:75
  92.6 0.1 dynamic_slice.10
  92.7 0.1 pad.3.clone
  92.8 12.8 %all-gather.6.cloned.1.call-done = bf16[512,1536]{1,0:T(8,128)(2,1)} async-done(((bf16[128,1536]{1,0:T(8,128)(2,1)}), bf16[512,1536]{1,0:T(8,128)(2,1)}) %all-gather.6.cloned.1.call-update) | async-done | bytes 1572880 | tf_op jit(solution)/shard_map/all_gather | solution.py:57
  105.6 2.3 %convert_reduce_fusion.2 = f32[1536]{0:T(1024)} fusion(bf16[512,1536]{1,0:T(8,128)(2,1)} %all-gather.6.cloned.1.call-done), kind=kLoop, calls=%fused_computation.11 | loop fusion | flops 1571328 | bytes 1579008 | tf_op jit(solution)/shard_map/reduce_sum | solution.py:123
  107.9 6.7 %convolution_convert_fusion = bf16[1536,1536]{1,0:T(8,128)(2,1)} fusion(bf16[512,1536]{1,0:T(8,128)(2,1)} %bitcast.12, bf16[512,1536]{1,0:T(8,128)(2,1)} %all-gather.6.cloned.1.call-done), kind=kOutput, calls=%fused_computation | convolution fusion | flops 2418278400 | bytes 7864320 | tf_op jit(solution)/shard_map/dot_general | solution.py:120
  114.6 16.5 %all-to-all-done.1 = bf16[8,784,128]{2,1,0:T(8,128)(2,1)S(1)} async-done(((bf16[8,784,128]{2,1,0:T(8,128)(2,1)}), bf16[8,784,128]{2,1,0:T(8,128)(2,1)S(1)}, u32[]{:S(2)}, u32[]{:S(2)}) %all-to-all-start.1) | async-done | bytes 1605664 | tf_op jit(solution)/shard_map/all_to_all | solution.py:75
  131.1 0.2 convert_reduce_fusion.1
  131.3 0.2 copy.26
  131.5 1.2 fusion.20
  132.7 0.1 maximum_maximum_fusion
  132.8 12.2 %all-gather = bf16[576,768]{1,0:T(8,128)(2,1)S(1)} all-gather(bf16[144,768]{1,0:T(8,128)(2,1)S(1)} %maximum_maximum_fusion), channel_id=2, replica_groups=mesh['dp'=4,'fsdp'=8] {'dp'}, dimensions={0}, use_global_device_ids=true | all-gather | bytes 1105920 | tf_op jit(solution)/shard_map/all_gather | solution.py:97
  145.0 0.1 slice.31
  145.0 0.6 convert_reduce_fusion.3
  145.7 1.3 convolution_convert_fusion.2
  (18 shorter events, 0.1 us)
Async XLA Ops:
  7.2 4.3 %copy-start = (bf16[384,768]{1,0:T(8,128)(2,1)S(1)}, bf16[384,768]{1,0:T(8,128)(2,1)}, u32[]{:S(2)}) copy-start(bf16[384,768]{1,0:T(8,128)(2,1)} %param.7) | copy-start | bytes 1769476
  7.2 47.0 %all-gather.4.cloned.1.call-start = ((), (), s32[]{:S(2)}) async-start(), calls=%async_computation.3 | async-start | bytes 1769472 | tf_op jit(solution)/shard_map/all_gather | solution.py:43
  12.1 45.9 %copy-start.3 = (f32[6144]{0:T(1024)S(1)}, f32[6144]{0:T(1024)}, u32[]{:S(2)}) copy-start(f32[6144]{0:T(1024)} %param.8) | copy-start | bytes 73732
  54.1 3.8 %copy-start.1 = (bf16[128,6144]{1,0:T(8,128)(2,1)S(1)}, bf16[128,6144]{1,0:T(8,128)(2,1)}, u32[]{:S(2)}) copy-start(bf16[128,6144]{1,0:T(8,128)(2,1)} %all-gather.4.cloned.1.call-done) | copy-start | bytes 4718596
  58.5 5.7 %copy-start.2 = (bf16[128,1536]{1,0:T(8,128)(2,1)S(1)}, bf16[128,1536]{1,0:T(8,128)(2,1)}, u32[]{:S(2)}) copy-start(bf16[128,1536]{1,0:T(8,128)(2,1)} %param.11) | copy-start | bytes 1179652
  58.5 5.7 %copy-start.4 = (f32[1536]{0:T(1024)S(1)}, f32[1536]{0:T(1024)}, u32[]{:S(2)}) copy-start(f32[1536]{0:T(1024)} %param.10) | copy-start | bytes 18436
  59.9 29.2 %all-to-all-start.2 = ((bf16[128,4,1536]{2,0,1:T(8,128)(2,1)}), bf16[128,4,1536]{2,0,1:T(8,128)(2,1)}, u32[]{:S(2)}, u32[]{:S(2)}) async-start(bf16[128,4,1536]{2,0,1:T(8,128)(2,1)} %bitcast.45), calls=%async_computation.2 | async-start | bytes 3145728 | tf_op jit(solution)/shard_map/all_to_all | solution.py:58
  64.2 41.4 %all-gather.6.cloned.1.call-start = ((), (), s32[]{:S(2)}) async-start(), calls=%async_computation.4 | async-start | bytes 1966080 | tf_op jit(solution)/shard_map/all_gather | solution.py:57
  89.0 42.0 %all-to-all-start.1 = ((bf16[8,784,128]{2,1,0:T(8,128)(2,1)}), bf16[8,784,128]{2,1,0:T(8,128)(2,1)S(1)}, u32[]{:S(2)}, u32[]{:S(2)}) async-start(bf16[8,784,128]{2,1,0:T(8,128)(2,1)} %pad_maximum_fusion), calls=%async_computation.1 | async-start | bytes 3211264 | tf_op jit(solution)/shard_map/all_to_all | solution.py:75
Sparse Core Ops, SparseCore 0:
  29.3 24.7 all-gather.3
  74.6 30.9 all-gather.5

commit v2 on v1

--- a/solution.py
+++ b/solution.py
@@ -1,6 +1,10 @@
+import functools
+
 import jax
 import jax.numpy as jnp
 from jax import lax
+from jax.experimental import pallas as pl
+from jax.experimental.pallas import tpu as pltpu
 from jax.sharding import PartitionSpec as P
 
 EPS = 1e-06
@@ -102,6 +106,243 @@
     return hidden, column_rows, piece, gradients, gain_gradient
 
 
+def fused_kernel(
+    groups, shards_of, outgoing, gain, bias, grad_hidden, w_hbm,
+    hidden, columns, pieces, back, gain_sums,
+    w_up, arrived, gathered, normed, sib_send, sib_recv, own, sum_send, sum_recv, stats,
+    send_sem, recv_sem, load_sem,
+):
+    group, shard = lax.axis_index("dp"), lax.axis_index("fsdp")
+    chip, core = shard // 2, lax.rem(shard, 2)
+    chips = shards_of // 2
+    sibling = shard + 1 - 2 * core
+    rows, width = outgoing.shape[1:]
+    full_width = shards_of * width
+    hidden_units = bias.shape[1]
+    counter = [0]
+    pending = []
+
+    def send(source, target, device):
+        index = counter[0]
+        counter[0] += 1
+        copy = pltpu.make_async_remote_copy(
+            src_ref=source,
+            dst_ref=target,
+            send_sem=send_sem.at[index],
+            recv_sem=recv_sem.at[index],
+            device_id=device,
+            device_id_type=pl.DeviceIdType.MESH,
+        )
+        copy.start()
+        pending.append(copy)
+        return copy
+
+    def other_group(step):
+        return lax.rem(group + step, groups)
+
+    def source_group(step):
+        return lax.rem(group - step + groups, groups)
+
+    load = pltpu.make_async_copy(w_hbm, w_up, load_sem)
+    load.start()
+    barrier = pltpu.get_barrier_semaphore()
+    for step in range(1, groups):
+        pl.semaphore_signal(barrier, inc=1, device_id={"dp": other_group(step)}, device_id_type=pl.DeviceIdType.MESH)
+    for step in range(1, shards_of):
+        pl.semaphore_signal(barrier, inc=1, device_id={"fsdp": lax.rem(shard + step, shards_of)}, device_id_type=pl.DeviceIdType.MESH)
+    pl.semaphore_wait(barrier, groups + shards_of - 2)
+
+    copies = [
+        send(outgoing.at[other_group(step)], arrived.at[step - 1], {"dp": other_group(step)})
+        for step in range(1, groups)
+    ]
+    packed = outgoing[group].astype(jnp.float32)
+    for step in range(1, groups):
+        copies[step - 1].wait_recv()
+        packed = packed + arrived[step - 1].astype(jnp.float32)
+    gathered[shard] = packed.astype(jnp.bfloat16)
+
+    copies = [
+        send(gathered.at[shard], gathered.at[shard], {"fsdp": lax.rem(chip + step, chips) * 2 + core})
+        for step in range(1, chips)
+    ]
+    forwards = [send(gathered.at[shard], gathered.at[shard], {"fsdp": sibling})]
+    for step in range(1, chips):
+        copies[step - 1].wait_recv()
+        came = lax.rem(chip - step + chips, chips) * 2 + core
+        forwards.append(send(gathered.at[came], gathered.at[came], {"fsdp": sibling}))
+    for copy in forwards:
+        copy.wait_recv()
+
+    total = jnp.zeros((rows, 1), jnp.float32)
+    for j in range(shards_of):
+        total = total + jnp.sum(gathered[j].astype(jnp.float32), axis=1, keepdims=True)
+    mean = total / full_width
+    total = jnp.zeros((rows, 1), jnp.float32)
+    for j in range(shards_of):
+        centred = gathered[j].astype(jnp.float32) - mean
+        total = total + jnp.sum(centred * centred, axis=1, keepdims=True)
+    inverse = lax.rsqrt(total / full_width + EPS)
+
+    def normalized(j):
+        return (gathered[j].astype(jnp.float32) - mean) * inverse
+
+    for j in range(shards_of):
+        normed[j] = (normalized(j) * gain[j]).astype(jnp.bfloat16)
+
+    half = pl.ds(pl.multiple_of(core * width, 128), width)
+    column_copies = [
+        send(normed.at[other_group(step) * 2 + core], columns.at[group, :, half], {"dp": other_group(step)})
+        for step in range(1, groups)
+    ]
+    columns[group, :, :width] = normed[2 * group]
+    columns[group, :, width:] = normed[2 * group + 1]
+
+    load.wait()
+
+    def forward(n, carry):
+        tile = pl.ds(pl.multiple_of(n * 256, 256), 256)
+        acc = jnp.zeros((rows, 256), jnp.float32)
+        for j in range(shards_of):
+            acc = acc + jnp.dot(
+                normed[j], w_up[j * width : (j + 1) * width, tile], preferred_element_type=jnp.float32
+            )
+        value, slope = gelu_parts(acc + bias[:, tile])
+        hidden[:, tile] = value.astype(jnp.bfloat16)
+        pieces[group, :, tile] = (grad_hidden[:, tile].astype(jnp.float32) * slope).astype(jnp.bfloat16)
+        return carry
+
+    lax.fori_loop(0, hidden_units // 256, forward, 0)
+    piece_copies = [
+        send(pieces.at[group], pieces.at[group], {"dp": other_group(step)}) for step in range(1, groups)
+    ]
+
+    def partial(j):
+        lanes = pl.ds(pl.multiple_of(j * width, 128), width)
+        return lax.dot_general(
+            pieces[group], w_up[lanes, :], (((1,), (1,)), ((), ())), preferred_element_type=jnp.float32
+        )
+
+    plain = jnp.zeros((rows, 1), jnp.float32)
+    weighted = jnp.zeros((rows, 1), jnp.float32)
+    sib_copies, sum_copies = [], []
+
+    def pass_on(i):
+        sib_copies[i].wait_recv()
+        sum_send[i] = (own[i] + sib_recv[i].astype(jnp.float32)).astype(jnp.bfloat16)
+        target = lax.rem(chip + 1 + i, chips) * 2 + core
+        sum_copies.append(send(sum_send.at[i], sum_recv.at[i], {"fsdp": target}))
+
+    for i in range(chips):
+        base = lax.rem(chip + 1 + i, chips) * 2
+        for mine in (False, True):
+            j = base + (core if mine else 1 - core)
+            part = partial(j)
+            scaled = part * gain[j]
+            plain = plain + jnp.sum(scaled, axis=1, keepdims=True)
+            weighted = weighted + jnp.sum(scaled * normalized(j), axis=1, keepdims=True)
+            if mine:
+                own[i] = part
+            else:
+                sib_send[i] = part.astype(jnp.bfloat16)
+                sib_copies.append(send(sib_send.at[i], sib_recv.at[i], {"fsdp": sibling}))
+        if i > 0:
+            pass_on(i - 1)
+
+    lane = lax.broadcasted_iota(jnp.int32, (rows, rows), 1)
+    both = jnp.where(lane == 0, plain, jnp.where(lane == 1, weighted, 0.0))
+    stats[shard] = both.T[:8]
+    stat_copies = [
+        send(stats.at[shard], stats.at[shard], {"fsdp": lax.rem(shard + step, shards_of)})
+        for step in range(1, shards_of)
+    ]
+    for step in range(1, groups):
+        column_copies[step - 1].wait_recv()
+        came = columns.at[source_group(step), :, half]
+        column_copies.append(send(came, came, {"fsdp": sibling}))
+
+    for copy in stat_copies:
+        copy.wait_recv()
+    summed = stats[0]
+    for j in range(1, shards_of):
+        summed = summed + stats[j]
+    upright = jnp.concatenate([summed, jnp.zeros((rows - 8, rows), jnp.float32)], axis=0).T
+    plain_mean = upright[:, 0:1] / full_width
+    weighted_mean = upright[:, 1:2] / full_width
+    sib_copies[chips - 1].wait_recv()
+    gradient = own[chips - 1] + sib_recv[chips - 1].astype(jnp.float32)
+    for i in range(chips - 1):
+        sum_copies[i].wait_recv()
+        gradient = gradient + sum_recv[i].astype(jnp.float32)
+    local = normalized(shard)
+    back[group] = (
+        inverse * (gradient * gain[shard] - plain_mean - local * weighted_mean)
+    ).astype(jnp.bfloat16)
+    gain_sums[group] = jnp.broadcast_to(jnp.sum(gradient * local, axis=0, keepdims=True), (8, width))
+    last = []
+    for step in range(1, groups):
+        device = {"dp": other_group(step)}
+        last.append(send(back.at[group], back.at[group], device))
+        last.append(send(gain_sums.at[group], gain_sums.at[group], device))
+    for copy in column_copies[groups - 1 :] + piece_copies + last:
+        copy.wait_recv()
+    for copy in pending:
+        copy.wait_send()
+
+
+def fused(outgoing, gain, w_up, bias, grad_hidden):
+    groups, rows, width = outgoing.shape
+    shards_of = lax.axis_size("fsdp")
+    hidden_units = bias.shape[0]
+    chips = shards_of // 2
+    bf16, f32 = jnp.bfloat16, jnp.float32
+    copies = 4 * (groups - 1) + 2 * (groups - 1) + 2 * (chips - 1) + 2 * chips + shards_of - 1
+    vmem = pl.BlockSpec(memory_space=pltpu.VMEM)
+    hidden, columns, pieces, back, gain_sums = pl.pallas_call(
+        functools.partial(fused_kernel, groups, shards_of),
+        out_shape=[
+            jax.ShapeDtypeStruct((rows, hidden_units), bf16),
+            jax.ShapeDtypeStruct((groups, rows, 2 * width), bf16),
+            jax.ShapeDtypeStruct((groups, rows, hidden_units), bf16),
+            jax.ShapeDtypeStruct((groups, rows, width), bf16),
+            jax.ShapeDtypeStruct((groups, 8, width), f32),
+        ],
+        in_specs=[vmem] * 4 + [pl.BlockSpec(memory_space=pl.ANY)],
+        out_specs=[vmem] * 5,
+        scratch_shapes=[
+            pltpu.VMEM(w_up.shape, bf16),
+            pltpu.VMEM((groups - 1, rows, width), bf16),
+            pltpu.VMEM((shards_of, rows, width), bf16),
+            pltpu.VMEM((shards_of, rows, width), bf16),
+            pltpu.VMEM((chips, rows, width), bf16),
+            pltpu.VMEM((chips, rows, width), bf16),
+            pltpu.VMEM((chips, rows, width), f32),
+            pltpu.VMEM((chips - 1, rows, width), bf16),
+            pltpu.VMEM((chips - 1, rows, width), bf16),
+            pltpu.VMEM((shards_of, 8, rows), f32),
+            pltpu.SemaphoreType.DMA((copies,)),
+            pltpu.SemaphoreType.DMA((copies,)),
+            pltpu.SemaphoreType.DMA,
+        ],
+        compiler_params=pltpu.CompilerParams(
+            collective_id=0, has_side_effects=True, vmem_limit_bytes=50 * 1024 * 1024
+        ),
+    )(outgoing, gain.reshape(shards_of, 1, width), bias[None], grad_hidden, w_up)
+    return (
+        hidden,
+        columns.reshape(groups * rows, 2 * width),
+        pieces.reshape(groups * rows, hidden_units),
+        back.reshape(groups * rows, width),
+        jnp.sum(gain_sums[:, 0], axis=0),
+    )
+
+
+def fits_tiles(groups, shards_of, rows, width, hidden_units):
+    return (
+        shards_of == 2 * groups and rows == 128 and width % 128 == 0 and hidden_units % 256 == 0
+    )
+
+
 def shards(patches, gain, w_up, bias, grad_hidden, patch_counts, image_source):
     groups, images = patch_counts.shape
     group_rows = grad_hidden.shape[0]
@@ -114,7 +355,11 @@
     placed = (rows[None, :] == numbers[:, None]).astype(jnp.bfloat16)
     outgoing = jnp.dot(placed, patches, preferred_element_type=jnp.float32)
     outgoing = outgoing.astype(jnp.bfloat16).reshape(groups, group_rows, local_width)
-    hidden, column_rows, piece, gradients, gain_gradient = middle(
+    tiled = fits_tiles(
+        groups, lax.axis_size("fsdp"), group_rows, local_width, grad_hidden.shape[1]
+    )
+    arrange = fused if tiled else middle
+    hidden, column_rows, piece, gradients, gain_gradient = arrange(
         outgoing, gain, w_up, bias, grad_hidden
     )
     grad_weight = lax.dot_general(

time: 154 us -> 91.8 us (0.60)
  Pallas kernels: 0 us -> 77.4 us
  waiting for transfers between devices: 54.2 us -> 0 us
  blocking collectives: 28.4 us -> 0 us
  matrix products: 30 us -> 6.15 us
  between operations: 14.3 us -> 0.71 us
  other arithmetic: 13.5 us -> 4 us
  starting transfers between devices: 8.01 us -> 0 us
  local copies, waits for them, and re-layouts: 5.44 us -> 3.21 us
    pallas_call x0 -> x1, Pallas kernels: none -> 77.4 us  [fused(): pl.pallas_call(functools.partial(fused_kernel, groups, shards_of), out_sh...]
    all_gather x2 -> x0, waiting for transfers between devices: 37.7 us -> none  [the longest x1 24.8 us: middle(): gathered = lax.all_gather(packed, 'fsdp', axis=1, tiled=True)]
    dot_general x2 -> x0, matrix products: 21.4 us -> none  [the longest x1 11.2 us: middle(): lax.dot_general(w_up, grad_pre, (((1,), (1,)), ((), ())), preferred_eleme...]
    all_to_all x2 -> x0, waiting for transfers between devices: 16.5 us -> none  [the longest x1 16.5 us: middle(): lax.all_to_all(sent, 'fsdp', split_axis=0, concat_axis=0, tiled=True)]
    all_to_all x1 -> x0, blocking collectives: 16.3 us -> none  [middle(): lax.all_to_all(outgoing, 'dp', split_axis=0, concat_axis=0, tiled=True)]
    all_gather x1 -> x0, blocking collectives: 12.2 us -> none  [middle(): all_back = lax.all_gather(back, 'dp', axis=0)]
    all_to_all x2 -> x0, starting transfers between devices: 7.93 us -> none  [the longest x1 4.35 us: middle(): lax.all_to_all(normed_input, 'dp', split_axis=1, concat_axis=0, tiled=True)]
    reduce_sum x5 -> x1, other arithmetic: 5.45 us -> 0.61 us  [fused(): jnp.sum(gain_sums[:, 0], axis=0)]
  transfers between devices with their start and end apart: 4 -> 0, of which waited for: 3 -> 0; matrix products, arithmetic and copies ran while one was open for 22% -> 0% of each run, Pallas kernels for 0% -> 0%
where the time goes in v2:
time: 91.8 us; the launch traced here: 91.5 us
  Pallas kernels  77.4 us (84%)
  matrix products  6.15 us (7%)
  other arithmetic  4 us (4%)
  local copies, waits for them, and re-layouts  3.21 us (3%)
    pallas_call x1, Pallas kernels, fused(): pl.pallas_call(functools.partial(fused_kernel, groups, shards_of), out_sh...  77.4 us
    dot_general x1, matrix products, shards(): lax.dot_general(column_rows, piece, (((0,), (0,)), ((), ())), preferred_e...  4.27 us

profile of v2, /device:TPU:0, one launch (start us, length us, event | category | flops | bytes accessed | tf_op | source)
XLA Modules:
  0.0 91.5 jit_solution(4178980656984413498)
XLA Ops:
  0.6 0.0 copy-start
  0.6 0.0 copy-start.1
  0.7 0.0 copy-start.2
  0.7 0.8 dynamic_slice.3
  1.5 0.8 broadcast_in_dim.36
  2.2 0.9 reduce_window_sum.11
  3.1 0.7 sub.8
  3.8 0.1 broadcast_in_dim.39
  3.9 0.2 select_reduce_fusion.1
  4.1 0.7 multiply_add_fusion
  4.8 0.1 add_select_fusion
  4.9 0.1 select_n.31
  5.0 0.7 broadcast_in_dim.42.bias
  5.7 0.0 copy-done
  5.7 0.6 convolution_convert_fusion
  6.2 0.0 copy-done.1
  6.2 0.0 copy-done.2
  6.2 77.4 %shard_map.110 = (bf16[128,1536]{1,0:T(8,128)(2,1)S(1)}, bf16[4,128,1536]{2,1,0:T(8,128)(2,1)S(1)}, bf16[4,128,1536]{2,1,0:T(8,128)(2,1)}, bf16[4,128,768]{2,1,0:T(8,128)(2,1)S(1)}, f32[4,8,768]{2,1,0:T(8,128)S(1)}) custom-call(bf16[4,128,768]{2,1,0:T(8,128)(2,1)S(1)} %bitcast.9, f32[8,1,768]{2,1,0:T(1,128)S(1)} %bitcast.10, ...), custom_call_target="tpu_custom_call" | custom-call | tf_op jit(solution)/shard_map/pallas_call | solution.py:301
  83.7 0.0 copy-start.3
  83.7 1.3 %convolution_convert_fusion.1 = bf16[384,768]{1,0:T(8,128)(2,1)} fusion(bf16[512,768]{1,0:T(8,128)(2,1)S(1)} %bitcast.11, s32[384]{0:T(512)S(1)} %select_n.31), kind=kOutput, calls=%fused_computation.3 | convolution fusion | flops 302481408 | bytes 1377792 | tf_op jit(solution)/shard_map/dot_general | solution.py:369
  85.0 0.6 slice_reduce_fusion
  85.6 0.0 copy-done.3
  85.6 0.9 convert_reduce_fusion
  86.5 4.3 %bitcast_convert_fusion = bf16[1536,1536]{1,0:T(8,128)(2,1)} fusion(bf16[4,128,1536]{2,1,0:T(8,128)(2,1)S(1)} %get-tuple-element.12, bf16[4,128,1536]{2,1,0:T(8,128)(2,1)S(1)} %copy-done.3), kind=kOutput, calls=%fused_computation | convolution fusion | flops 2418278400 | bytes 7864320 | tf_op jit(solution)/shard_map/dot_general | solution.py:365
  90.7 0.7 copy.16
Async XLA Ops:
  0.6 5.0 %copy-start = (bf16[384,768]{1,0:T(8,128)(2,1)S(1)}, bf16[384,768]{1,0:T(8,128)(2,1)}, u32[]{:S(2)}) copy-start(bf16[384,768]{1,0:T(8,128)(2,1)} %param.7) | copy-start | bytes 1769476
  0.6 5.6 %copy-start.1 = (bf16[128,1536]{1,0:T(8,128)(2,1)S(1)}, bf16[128,1536]{1,0:T(8,128)(2,1)}, u32[]{:S(2)}) copy-start(bf16[128,1536]{1,0:T(8,128)(2,1)} %grad_hidden.1) | copy-start | bytes 1179652
  0.7 5.6 %copy-start.2 = (f32[6144]{0:T(1024)S(1)}, f32[6144]{0:T(1024)}, u32[]{:S(2)}) copy-start(f32[6144]{0:T(1024)} %param.8) | copy-start | bytes 73732
  83.7 2.0 %copy-start.3 = (bf16[4,128,1536]{2,1,0:T(8,128)(2,1)S(1)}, bf16[4,128,1536]{2,1,0:T(8,128)(2,1)}, u32[]{:S(2)}) copy-start(bf16[4,128,1536]{2,1,0:T(8,128)(2,1)} %get-tuple-element.13) | copy-start | bytes 4718596

commit v3 on v2

--- a/solution.py
+++ b/solution.py
@@ -8,6 +8,7 @@
 from jax.sharding import PartitionSpec as P
 
 EPS = 1e-06
+PARTS = 4
 ROOT_HALF = 0.7071067811865476
 INV_ROOT_TAU = 0.3989422804014327
 
@@ -20,13 +21,13 @@
 
 def destination_rows(patch_counts, image_source, group_index, group_rows, capacity):
     groups, images = patch_counts.shape
-    total_images = groups * images
-    starts = (jnp.cumsum(patch_counts, axis=1) - patch_counts).reshape(total_images)
-    lengths = patch_counts.reshape(total_images)
+    numbers = jnp.arange(groups * images, dtype=jnp.int32)[None, :]
+    lengths = patch_counts.reshape(1, groups * images)
     mine = lax.dynamic_slice_in_dim(image_source, group_index * images, images, 0)
-    chosen = mine[:, None] == jnp.arange(total_images, dtype=jnp.int32)[None, :]
-    start = jnp.sum(jnp.where(chosen, starts[None, :], 0), axis=1)
-    count = jnp.sum(jnp.where(chosen, lengths[None, :], 0), axis=1)
+    image = mine[:, None]
+    before = (numbers // images == image // images) & (numbers < image)
+    start = jnp.sum(jnp.where(before, lengths, 0), axis=1)
+    count = jnp.sum(jnp.where(numbers == image, lengths, 0), axis=1)
     offsets = jnp.arange(capacity, dtype=jnp.int32)
     first = (mine // images) * group_rows + start
     rows = jnp.where(offsets[None, :] < count[:, None], first[:, None] + offsets[None, :], -1)
@@ -109,7 +110,7 @@
 def fused_kernel(
     groups, shards_of, outgoing, gain, bias, grad_hidden, w_hbm,
     hidden, columns, pieces, back, gain_sums,
-    w_up, arrived, gathered, normed, sib_send, sib_recv, own, sum_send, sum_recv, stats,
+    w_up, arrived, gathered, normed, sib_send, sib_recv, own, sum_send, sum_recv, stats, means, squares,
     send_sem, recv_sem, load_sem,
 ):
     group, shard = lax.axis_index("dp"), lax.axis_index("fsdp")
@@ -122,7 +123,7 @@
     counter = [0]
     pending = []
 
-    def send(source, target, device):
+    def send(source, target, device, when=None):
         index = counter[0]
         counter[0] += 1
         copy = pltpu.make_async_remote_copy(
@@ -133,8 +134,11 @@
             device_id=device,
             device_id_type=pl.DeviceIdType.MESH,
         )
-        copy.start()
-        pending.append(copy)
+        if when is None:
+            copy.start()
+        else:
+            pl.when(when)(copy.start)
+        pending.append((copy, when))
         return copy
 
     def other_group(step):
@@ -152,36 +156,92 @@
         pl.semaphore_signal(barrier, inc=1, device_id={"fsdp": lax.rem(shard + step, shards_of)}, device_id_type=pl.DeviceIdType.MESH)
     pl.semaphore_wait(barrier, groups + shards_of - 2)
 
-    copies = [
-        send(outgoing.at[other_group(step)], arrived.at[step - 1], {"dp": other_group(step)})
-        for step in range(1, groups)
+    depth = rows // PARTS
+    spans = [pl.ds(h * depth, depth) for h in range(PARTS)]
+    row_copies = [
+        [
+            send(
+                outgoing.at[other_group(step), span],
+                arrived.at[step - 1, span],
+                {"dp": other_group(step)},
+            )
+            for step in range(1, groups)
+        ]
+        for span in spans
     ]
-    packed = outgoing[group].astype(jnp.float32)
-    for step in range(1, groups):
-        copies[step - 1].wait_recv()
-        packed = packed + arrived[step - 1].astype(jnp.float32)
-    gathered[shard] = packed.astype(jnp.bfloat16)
-
-    copies = [
-        send(gathered.at[shard], gathered.at[shard], {"fsdp": lax.rem(chip + step, chips) * 2 + core})
-        for step in range(1, chips)
-    ]
-    forwards = [send(gathered.at[shard], gathered.at[shard], {"fsdp": sibling})]
+
+    right_chip = {"fsdp": lax.rem(chip + 1, chips) * 2 + core}
+    left_chip = {"fsdp": lax.rem(chip + chips - 1, chips) * 2 + core}
+    beside = {"fsdp": sibling}
+    has_right, has_left = chip < chips - 1, chip > 0
+
+    def spread(j, span, device, when=None):
+        return send(gathered.at[j, span], gathered.at[j, span], device, when)
+
+    def row_statistics(j):
+        values = gathered[j].astype(jnp.float32)
+        mean = jnp.sum(values, axis=1, keepdims=True) / width
+        means[j] = mean
+        squares[j] = jnp.sum((values - mean) * (values - mean), axis=1, keepdims=True)
+
+    def other_core(j):
+        return j + 1 - 2 * core
+
+    rightward, leftward, own_beside = [], [], []
+    for h, span in enumerate(spans):
+        packed = outgoing[group, span].astype(jnp.float32)
+        for step in range(1, groups):
+            row_copies[h][step - 1].wait_recv()
+            packed = packed + arrived[step - 1, span].astype(jnp.float32)
+        gathered[shard, span] = packed.astype(jnp.bfloat16)
+        rightward.append(spread(shard, span, right_chip, has_right))
+        leftward.append(spread(shard, span, left_chip, has_left))
+        own_beside.append(spread(shard, span, beside))
+    row_statistics(shard)
+    waiting = [(None, other_core(shard), own_beside)]
+
+    def take_beside(when, j, copies):
+        def take():
+            for copy in copies:
+                copy.wait_recv()
+            row_statistics(j)
+
+        if when is None:
+            take()
+        else:
+            pl.when(when)(take)
+
     for step in range(1, chips):
-        copies[step - 1].wait_recv()
-        came = lax.rem(chip - step + chips, chips) * 2 + core
-        forwards.append(send(gathered.at[came], gathered.at[came], {"fsdp": sibling}))
-    for copy in forwards:
-        copy.wait_recv()
-
+        streams = [
+            (chip >= step, has_right, right_chip, lax.rem(chip - step + chips, chips), rightward),
+            (chip + step < chips, has_left, left_chip, lax.rem(chip + step, chips), leftward),
+        ]
+        besides = [[], []]
+        for h, span in enumerate(spans):
+            for side, (here, onward, device, came, stream) in enumerate(streams):
+                j = came * 2 + core
+                pl.when(here)(stream[h].wait_recv)
+                if step < chips - 1:
+                    stream[h] = spread(j, span, device, jnp.logical_and(here, onward))
+                besides[side].append(spread(j, span, beside, here))
+        for entry in waiting:
+            take_beside(*entry)
+        waiting = []
+        for side, (here, onward, device, came, stream) in enumerate(streams):
+            j = came * 2 + core
+            pl.when(here)(functools.partial(row_statistics, j))
+            waiting.append((here, other_core(j), besides[side]))
+    for entry in waiting:
+        take_beside(*entry)
+
+    mean = means[0]
+    for j in range(1, shards_of):
+        mean = mean + means[j]
+    mean = mean / shards_of
     total = jnp.zeros((rows, 1), jnp.float32)
     for j in range(shards_of):
-        total = total + jnp.sum(gathered[j].astype(jnp.float32), axis=1, keepdims=True)
-    mean = total / full_width
-    total = jnp.zeros((rows, 1), jnp.float32)
-    for j in range(shards_of):
-        centred = gathered[j].astype(jnp.float32) - mean
-        total = total + jnp.sum(centred * centred, axis=1, keepdims=True)
+        offset = means[j] - mean
+        total = total + squares[j] + width * (offset * offset)
     inverse = lax.rsqrt(total / full_width + EPS)
 
     def normalized(j):
@@ -286,8 +346,11 @@
         last.append(send(gain_sums.at[group], gain_sums.at[group], device))
     for copy in column_copies[groups - 1 :] + piece_copies + last:
         copy.wait_recv()
-    for copy in pending:
-        copy.wait_send()
+    for copy, when in pending:
+        if when is None:
+            copy.wait_send()
+        else:
+            pl.when(when)(copy.wait_send)
 
 
 def fused(outgoing, gain, w_up, bias, grad_hidden):
@@ -296,7 +359,9 @@
     hidden_units = bias.shape[0]
     chips = shards_of // 2
     bf16, f32 = jnp.bfloat16, jnp.float32
-    copies = 4 * (groups - 1) + 2 * (groups - 1) + 2 * (chips - 1) + 2 * chips + shards_of - 1
+    copies = (
+        (PARTS + 5) * (groups - 1) + PARTS * (4 * chips - 3) + 2 * chips - 1 + shards_of - 1
+    )
     vmem = pl.BlockSpec(memory_space=pltpu.VMEM)
     hidden, columns, pieces, back, gain_sums = pl.pallas_call(
         functools.partial(fused_kernel, groups, shards_of),
@@ -320,6 +385,8 @@
             pltpu.VMEM((chips - 1, rows, width), bf16),
             pltpu.VMEM((chips - 1, rows, width), bf16),
             pltpu.VMEM((shards_of, 8, rows), f32),
+            pltpu.VMEM((shards_of, rows, 1), f32),
+            pltpu.VMEM((shards_of, rows, 1), f32),
             pltpu.SemaphoreType.DMA((copies,)),
             pltpu.SemaphoreType.DMA((copies,)),
             pltpu.SemaphoreType.DMA,

time: 91.8 us -> 82.5 us (0.90)
  Pallas kernels: 77.4 us -> 69.8 us
  other arithmetic: 4 us -> 2.5 us
    pallas_call x1, Pallas kernels: 77.4 us -> 69.8 us  [fused(): pl.pallas_call(functools.partial(fused_kernel, groups, shards_of), out_sh...]
where the time goes in v3:
time: 82.5 us; the launch traced here: 82.3 us
  Pallas kernels  69.8 us (85%)
  matrix products  6.15 us (7%)
  local copies, waits for them, and re-layouts  3.13 us (4%)
  other arithmetic  2.5 us (3%)
    pallas_call x1, Pallas kernels, fused(): pl.pallas_call(functools.partial(fused_kernel, groups, shards_of), out_sh...  69.8 us
    dot_general x1, matrix products, shards(): lax.dot_general(column_rows, piece, (((0,), (0,)), ((), ())), preferred_e...  4.27 us

profile of v3, /device:TPU:0, one launch (start us, length us, event | category | flops | bytes accessed | tf_op | source)
XLA Modules:
  0.0 82.3 jit_solution(8267840756958401489)
XLA Ops:
  0.6 0.0 copy-start
  0.6 0.0 copy-start.1
  0.7 0.8 %broadcast_in_dim.32 = s32[32]{0:T(128)S(1)} reshape(s32[4,8]{1,0:T(4,128)} %param.12) | data formatting | bytes 256 | tf_op jit(solution)/shard_map/jit(_where)/broadcast_in_dim | solution.py:30
  1.5 0.7 and_select_fusion.1
  2.2 0.2 select_reduce_fusion.1
  2.5 0.1 add_select_fusion
  2.5 0.1 select_n.46
  2.6 0.7 broadcast_in_dim.36.bias
  3.3 0.0 copy-done
  3.3 0.6 convolution_convert_fusion
  3.9 0.0 copy-done.1
  3.9 0.0 copy-start.2
  3.9 0.7 copy-done.2
  4.7 69.8 %shard_map.110 = (bf16[128,1536]{1,0:T(8,128)(2,1)S(1)}, bf16[4,128,1536]{2,1,0:T(8,128)(2,1)S(1)}, bf16[4,128,1536]{2,1,0:T(8,128)(2,1)}, bf16[4,128,768]{2,1,0:T(8,128)(2,1)S(1)}, f32[4,8,768]{2,1,0:T(8,128)S(1)}) custom-call(bf16[4,128,768]{2,1,0:T(8,128)(2,1)S(1)} %bitcast.9, f32[8,1,768]{2,1,0:T(1,128)S(1)} %bitcast.10, ...), custom_call_target="tpu_custom_call" | custom-call | tf_op jit(solution)/shard_map/pallas_call | solution.py:366
  74.4 0.0 copy-start.3
  74.4 1.3 %convolution_convert_fusion.1 = bf16[384,768]{1,0:T(8,128)(2,1)} fusion(bf16[512,768]{1,0:T(8,128)(2,1)S(1)} %bitcast.11, s32[384]{0:T(512)S(1)} %select_n.46), kind=kOutput, calls=%fused_computation.3 | convolution fusion | flops 302481408 | bytes 1377792 | tf_op jit(solution)/shard_map/dot_general | solution.py:436
  75.8 0.6 slice_reduce_fusion
  76.4 0.0 copy-done.3
  76.4 0.9 %convert_reduce_fusion = f32[1536]{0:T(1024)} fusion(bf16[4,128,1536]{2,1,0:T(8,128)(2,1)S(1)} %copy-done.3), kind=kLoop, calls=%fused_computation.1 | loop fusion | flops 1571328 | bytes 1579008 | tf_op jit(solution)/shard_map/reduce_sum | solution.py:435
  77.2 4.3 %bitcast_convert_fusion = bf16[1536,1536]{1,0:T(8,128)(2,1)} fusion(bf16[4,128,1536]{2,1,0:T(8,128)(2,1)S(1)} %get-tuple-element.12, bf16[4,128,1536]{2,1,0:T(8,128)(2,1)S(1)} %copy-done.3), kind=kOutput, calls=%fused_computation | convolution fusion | flops 2418278400 | bytes 7864320 | tf_op jit(solution)/shard_map/dot_general | solution.py:432
  81.5 0.7 copy.16
  (2 shorter events, 0.0 us)
Async XLA Ops:
  0.6 2.7 %copy-start = (bf16[384,768]{1,0:T(8,128)(2,1)S(1)}, bf16[384,768]{1,0:T(8,128)(2,1)}, u32[]{:S(2)}) copy-start(bf16[384,768]{1,0:T(8,128)(2,1)} %param.7) | copy-start | bytes 1769476
  0.6 3.3 %copy-start.1 = (bf16[128,1536]{1,0:T(8,128)(2,1)S(1)}, bf16[128,1536]{1,0:T(8,128)(2,1)}, u32[]{:S(2)}) copy-start(bf16[128,1536]{1,0:T(8,128)(2,1)} %grad_hidden.1) | copy-start | bytes 1179652
  3.9 0.7 copy-start.2
  74.4 2.0 %copy-start.3 = (bf16[4,128,1536]{2,1,0:T(8,128)(2,1)S(1)}, bf16[4,128,1536]{2,1,0:T(8,128)(2,1)}, u32[]{:S(2)}) copy-start(bf16[4,128,1536]{2,1,0:T(8,128)(2,1)} %get-tuple-element.13) | copy-start | bytes 4718596

commit v4 on v3

--- a/solution.py
+++ b/solution.py
@@ -104,13 +104,17 @@
         all_back[:, group_rows : group_rows + 2].astype(jnp.float32), axis=(0, 1)
     )
     gradients = all_back[:, :group_rows].reshape(groups * group_rows, local_width)
-    return hidden, column_rows, piece, gradients, gain_gradient
+    grad_weight = lax.dot_general(
+        column_rows, piece, (((0,), (0,)), ((), ())), preferred_element_type=jnp.float32
+    ).astype(jnp.bfloat16)
+    grad_bias = jnp.sum(piece.astype(jnp.float32), axis=0)
+    return hidden, grad_weight, grad_bias, gradients, gain_gradient
 
 
 def fused_kernel(
     groups, shards_of, outgoing, gain, bias, grad_hidden, w_hbm,
-    hidden, columns, pieces, back, gain_sums,
-    w_up, arrived, gathered, normed, sib_send, sib_recv, own, sum_send, sum_recv, stats, means, squares,
+    hidden, grad_weight, grad_bias, back, gain_sums,
+    columns, pieces, w_up, arrived, gathered, normed, sib_send, sib_recv, own, sum_send, sum_recv, stats, means, squares,
     send_sem, recv_sem, load_sem,
 ):
     group, shard = lax.axis_index("dp"), lax.axis_index("fsdp")
@@ -285,13 +289,21 @@
 
     plain = jnp.zeros((rows, 1), jnp.float32)
     weighted = jnp.zeros((rows, 1), jnp.float32)
-    sib_copies, sum_copies = [], []
+    sib_copies, sum_copies = [], {}
+    halves = [pl.ds(h * (rows // 2), rows // 2) for h in range(2)]
 
     def pass_on(i):
         sib_copies[i].wait_recv()
         sum_send[i] = (own[i] + sib_recv[i].astype(jnp.float32)).astype(jnp.bfloat16)
+        pass_half(i, 0)
+        if i == 0:
+            pass_half(i, 1)
+
+    def pass_half(i, h):
         target = lax.rem(chip + 1 + i, chips) * 2 + core
-        sum_copies.append(send(sum_send.at[i], sum_recv.at[i], {"fsdp": target}))
+        sum_copies[i, h] = send(
+            sum_send.at[i, halves[h]], sum_recv.at[i, halves[h]], {"fsdp": target}
+        )
 
     for i in range(chips):
         base = lax.rem(chip + 1 + i, chips) * 2
@@ -309,6 +321,8 @@
         if i > 0:
             pass_on(i - 1)
 
+    for i in range(1, chips - 1):
+        pass_half(i, 1)
     lane = lax.broadcasted_iota(jnp.int32, (rows, rows), 1)
     both = jnp.where(lane == 0, plain, jnp.where(lane == 1, weighted, 0.0))
     stats[shard] = both.T[:8]
@@ -330,21 +344,46 @@
     plain_mean = upright[:, 0:1] / full_width
     weighted_mean = upright[:, 1:2] / full_width
     sib_copies[chips - 1].wait_recv()
-    gradient = own[chips - 1] + sib_recv[chips - 1].astype(jnp.float32)
-    for i in range(chips - 1):
-        sum_copies[i].wait_recv()
-        gradient = gradient + sum_recv[i].astype(jnp.float32)
-    local = normalized(shard)
-    back[group] = (
-        inverse * (gradient * gain[shard] - plain_mean - local * weighted_mean)
-    ).astype(jnp.bfloat16)
-    gain_sums[group] = jnp.broadcast_to(jnp.sum(gradient * local, axis=0, keepdims=True), (8, width))
+    gain_sum = jnp.zeros((1, width), jnp.float32)
     last = []
+    for h, span in enumerate(halves):
+        here = slice(h * (rows // 2), (h + 1) * (rows // 2))
+        gradient = own[chips - 1, span] + sib_recv[chips - 1, span].astype(jnp.float32)
+        for i in range(chips - 1):
+            sum_copies[i, h].wait_recv()
+            gradient = gradient + sum_recv[i, span].astype(jnp.float32)
+        local = (gathered[shard, span].astype(jnp.float32) - mean[here]) * inverse[here]
+        back[group, span] = (
+            inverse[here] * (gradient * gain[shard] - plain_mean[here] - local * weighted_mean[here])
+        ).astype(jnp.bfloat16)
+        gain_sum = gain_sum + jnp.sum(gradient * local, axis=0, keepdims=True)
+        for step in range(1, groups):
+            device = {"dp": other_group(step)}
+            last.append(send(back.at[group, span], back.at[group, span], device))
+    gain_sums[group] = jnp.broadcast_to(gain_sum, (8, width))
     for step in range(1, groups):
-        device = {"dp": other_group(step)}
-        last.append(send(back.at[group], back.at[group], device))
-        last.append(send(gain_sums.at[group], gain_sums.at[group], device))
-    for copy in column_copies[groups - 1 :] + piece_copies + last:
+        last.append(send(gain_sums.at[group], gain_sums.at[group], {"dp": other_group(step)}))
+
+    for copy in column_copies[groups - 1 :] + piece_copies:
+        copy.wait_recv()
+
+    def weight_rows(n, carry):
+        tile = pl.ds(pl.multiple_of(n * 256, 256), 256)
+        all_pieces = pieces[...].reshape(groups * rows, hidden_units)
+        grad_weight[tile, :] = lax.dot_general(
+            columns[:, :, tile].reshape(groups * rows, 256),
+            all_pieces,
+            (((0,), (0,)), ((), ())),
+            preferred_element_type=jnp.float32,
+        ).astype(jnp.bfloat16)
+        return carry
+
+    lax.fori_loop(0, 2 * width // 256, weight_rows, 0)
+    bias_sum = jnp.zeros((1, hidden_units), jnp.float32)
+    for j in range(groups):
+        bias_sum = bias_sum + jnp.sum(pieces[j].astype(jnp.float32), axis=0, keepdims=True)
+    grad_bias[...] = bias_sum
+    for copy in last:
         copy.wait_recv()
     for copy, when in pending:
         if when is None:
@@ -360,21 +399,23 @@
     chips = shards_of // 2
     bf16, f32 = jnp.bfloat16, jnp.float32
     copies = (
-        (PARTS + 5) * (groups - 1) + PARTS * (4 * chips - 3) + 2 * chips - 1 + shards_of - 1
+        (PARTS + 6) * (groups - 1) + PARTS * (4 * chips - 3) + 3 * chips - 2 + shards_of - 1
     )
     vmem = pl.BlockSpec(memory_space=pltpu.VMEM)
-    hidden, columns, pieces, back, gain_sums = pl.pallas_call(
+    hidden, grad_weight, grad_bias, back, gain_sums = pl.pallas_call(
         functools.partial(fused_kernel, groups, shards_of),
         out_shape=[
             jax.ShapeDtypeStruct((rows, hidden_units), bf16),
-            jax.ShapeDtypeStruct((groups, rows, 2 * width), bf16),
-            jax.ShapeDtypeStruct((groups, rows, hidden_units), bf16),
+            jax.ShapeDtypeStruct((2 * width, hidden_units), bf16),
+            jax.ShapeDtypeStruct((1, hidden_units), f32),
             jax.ShapeDtypeStruct((groups, rows, width), bf16),
             jax.ShapeDtypeStruct((groups, 8, width), f32),
         ],
         in_specs=[vmem] * 4 + [pl.BlockSpec(memory_space=pl.ANY)],
         out_specs=[vmem] * 5,
         scratch_shapes=[
+            pltpu.VMEM((groups, rows, 2 * width), bf16),
+            pltpu.VMEM((groups, rows, hidden_units), bf16),
             pltpu.VMEM(w_up.shape, bf16),
             pltpu.VMEM((groups - 1, rows, width), bf16),
             pltpu.VMEM((shards_of, rows, width), bf16),
@@ -397,8 +438,8 @@
     )(outgoing, gain.reshape(shards_of, 1, width), bias[None], grad_hidden, w_up)
     return (
         hidden,
-        columns.reshape(groups * rows, 2 * width),
-        pieces.reshape(groups * rows, hidden_units),
+        grad_weight,
+        grad_bias[0],
         back.reshape(groups * rows, width),
         jnp.sum(gain_sums[:, 0], axis=0),
     )
@@ -426,13 +467,9 @@
         groups, lax.axis_size("fsdp"), group_rows, local_width, grad_hidden.shape[1]
     )
     arrange = fused if tiled else middle
-    hidden, column_rows, piece, gradients, gain_gradient = arrange(
+    hidden, grad_weight, grad_bias, gradients, gain_gradient = arrange(
         outgoing, gain, w_up, bias, grad_hidden
     )
-    grad_weight = lax.dot_general(
-        column_rows, piece, (((0,), (0,)), ((), ())), preferred_element_type=jnp.float32
-    ).astype(jnp.bfloat16)
-    grad_bias = jnp.sum(piece.astype(jnp.float32), axis=0)
     grad_patches = lax.dot_general(
         placed, gradients, (((0,), (0,)), ((), ())), preferred_element_type=jnp.float32
     ).astype(jnp.bfloat16)

time: 82.5 us -> 84.7 us (1.027)
  local copies, waits for them, and re-layouts: 3.13 us -> 8.93 us
  matrix products: 6.15 us -> 1.89 us
  Pallas kernels: 69.8 us -> 70.7 us
    unnamed x9 -> x8, local copies, waits for them, and re-layouts: 1.5 us -> 7.31 us
    dot_general x1 -> x0, matrix products: 4.27 us -> none  [shards(): lax.dot_general(column_rows, piece, (((0,), (0,)), ((), ())), preferred_e...]
    pallas_call x1, Pallas kernels: 69.8 us -> 70.7 us  [fused(): pl.pallas_call(functools.partial(fused_kernel, groups, shards_of), out_sh...]
    reduce_sum x1 -> x0, other arithmetic: 0.86 us -> none  [shards(): grad_bias = jnp.sum(piece.astype(jnp.float32), axis=0)]
where the time goes in v4:
time: 84.7 us; the launch traced here: 84.4 us
  Pallas kernels  70.7 us (83%)
  local copies, waits for them, and re-layouts  8.93 us (11%)
  other arithmetic  2.26 us (3%)
  matrix products  1.89 us (2%)
    pallas_call x1, Pallas kernels, fused(): pl.pallas_call(functools.partial(fused_kernel, groups, shards_of), out_sh...  70.7 us
    unnamed x8, local copies, waits for them, and re-layouts  7.31 us

profile of v4, /device:TPU:0, one launch (start us, length us, event | category | flops | bytes accessed | tf_op | source)
XLA Modules:
  0.0 84.4 jit_solution(13717751002260115247)
XLA Ops:
  0.6 0.0 copy-start
  0.7 0.8 broadcast_in_dim.32
  1.5 0.7 and_select_fusion.1
  2.2 0.2 select_reduce_fusion.1
  2.4 0.1 add_select_fusion
  2.5 0.1 select_n.46
  2.6 0.7 broadcast_in_dim.36.bias
  3.3 0.0 copy-done
  3.3 0.6 convolution_convert_fusion
  3.9 0.0 copy-start.1
  3.9 1.0 %copy-done.1 = bf16[128,1536]{1,0:T(8,128)(2,1)S(1)} copy-done((bf16[128,1536]{1,0:T(8,128)(2,1)S(1)}, bf16[128,1536]{1,0:T(8,128)(2,1)}, u32[]{:S(2)}) %copy-start.1) | copy-done | bytes 393240
  4.9 0.0 copy-start.2
  4.9 0.7 copy-done.2
  5.6 70.7 %shard_map.110 = (bf16[128,1536]{1,0:T(8,128)(2,1)S(1)}, bf16[1536,1536]{1,0:T(8,128)(2,1)}, f32[1,1536]{1,0:T(1,128)S(1)}, bf16[4,128,768]{2,1,0:T(8,128)(2,1)S(1)}, f32[4,8,768]{2,1,0:T(8,128)S(1)}) custom-call(bf16[4,128,768]{2,1,0:T(8,128)(2,1)S(1)} %bitcast.5, f32[8,1,768]{2,1,0:T(1,128)S(1)} %bitcast.6, f32[1,1536]{1,0:T(1,128)S(1)} %broadcast_in_dim.36.bias, ...), custom_call_target="tpu_custom_call" | custom-call | tf_op jit(solution)/shard_map/pallas_call | solution.py:405
  76.3 1.3 %convolution_convert_fusion.1 = bf16[384,768]{1,0:T(8,128)(2,1)} fusion(bf16[512,768]{1,0:T(8,128)(2,1)S(1)} %bitcast.7, s32[384]{0:T(512)S(1)} %select_n.46), kind=kOutput, calls=%fused_computation.1 | convolution fusion | flops 302481408 | bytes 1377792 | tf_op jit(solution)/shard_map/dot_general | solution.py:473
  77.6 0.6 slice_reduce_fusion
  78.2 0.6 reduce.1
  78.9 0.7 copy.14
  79.6 4.8 %copy.15 = bf16[1536,1536]{1,0:T(8,128)(2,1)} copy(bf16[1536,1536]{1,0:T(8,128)(2,1)} %get-tuple-element.26) | data formatting | bytes 9437184
  (2 shorter events, 0.0 us)
Async XLA Ops:
  0.6 2.7 %copy-start = (bf16[384,768]{1,0:T(8,128)(2,1)S(1)}, bf16[384,768]{1,0:T(8,128)(2,1)}, u32[]{:S(2)}) copy-start(bf16[384,768]{1,0:T(8,128)(2,1)} %param.7) | copy-start | bytes 1769476
  3.9 1.0 %copy-start.1 = (bf16[128,1536]{1,0:T(8,128)(2,1)S(1)}, bf16[128,1536]{1,0:T(8,128)(2,1)}, u32[]{:S(2)}) copy-start(bf16[128,1536]{1,0:T(8,128)(2,1)} %grad_hidden.1) | copy-start | bytes 1179652
  4.9 0.7 copy-start.2

commit v5 on v4

--- a/solution.py
+++ b/solution.py
@@ -38,6 +38,13 @@
     high = values.astype(jnp.bfloat16)
     low = (values - high.astype(jnp.float32)).astype(jnp.bfloat16)
     return high, low
+
+
+def weight_gradients(column_rows, piece):
+    grad_weight = lax.dot_general(
+        column_rows, piece, (((0,), (0,)), ((), ())), preferred_element_type=jnp.float32
+    ).astype(jnp.bfloat16)
+    return grad_weight, jnp.sum(piece.astype(jnp.float32), axis=0)
 
 
 def middle(outgoing, gain, w_up, bias, grad_hidden):
@@ -104,18 +111,14 @@
         all_back[:, group_rows : group_rows + 2].astype(jnp.float32), axis=(0, 1)
     )
     gradients = all_back[:, :group_rows].reshape(groups * group_rows, local_width)
-    grad_weight = lax.dot_general(
-        column_rows, piece, (((0,), (0,)), ((), ())), preferred_element_type=jnp.float32
-    ).astype(jnp.bfloat16)
-    grad_bias = jnp.sum(piece.astype(jnp.float32), axis=0)
-    return hidden, grad_weight, grad_bias, gradients, gain_gradient
+    return hidden, *weight_gradients(column_rows, piece), gradients, gain_gradient
 
 
 def fused_kernel(
-    groups, shards_of, outgoing, gain, bias, grad_hidden, w_hbm,
-    hidden, grad_weight, grad_bias, back, gain_sums,
-    columns, pieces, w_up, arrived, gathered, normed, sib_send, sib_recv, own, sum_send, sum_recv, stats, means, squares,
-    send_sem, recv_sem, load_sem,
+    groups, shards_of, outgoing, gain, bias, grad_hidden_hbm, w_hbm,
+    hidden, columns, pieces, back, gain_sums,
+    grad_hidden, w_up, arrived, gathered, normed, sib_send, sib_recv, own, sum_send, sum_recv, stats, means, squares,
+    send_sem, recv_sem, load_sem, small_load_sem,
 ):
     group, shard = lax.axis_index("dp"), lax.axis_index("fsdp")
     chip, core = shard // 2, lax.rem(shard, 2)
@@ -153,6 +156,8 @@
 
     load = pltpu.make_async_copy(w_hbm, w_up, load_sem)
     load.start()
+    small_load = pltpu.make_async_copy(grad_hidden_hbm, grad_hidden, small_load_sem)
+    small_load.start()
     barrier = pltpu.get_barrier_semaphore()
     for step in range(1, groups):
         pl.semaphore_signal(barrier, inc=1, device_id={"dp": other_group(step)}, device_id_type=pl.DeviceIdType.MESH)
@@ -263,6 +268,7 @@
     columns[group, :, width:] = normed[2 * group + 1]
 
     load.wait()
+    small_load.wait()
 
     def forward(n, carry):
         tile = pl.ds(pl.multiple_of(n * 256, 256), 256)
@@ -367,22 +373,6 @@
     for copy in column_copies[groups - 1 :] + piece_copies:
         copy.wait_recv()
 
-    def weight_rows(n, carry):
-        tile = pl.ds(pl.multiple_of(n * 256, 256), 256)
-        all_pieces = pieces[...].reshape(groups * rows, hidden_units)
-        grad_weight[tile, :] = lax.dot_general(
-            columns[:, :, tile].reshape(groups * rows, 256),
-            all_pieces,
-            (((0,), (0,)), ((), ())),
-            preferred_element_type=jnp.float32,
-        ).astype(jnp.bfloat16)
-        return carry
-
-    lax.fori_loop(0, 2 * width // 256, weight_rows, 0)
-    bias_sum = jnp.zeros((1, hidden_units), jnp.float32)
-    for j in range(groups):
-        bias_sum = bias_sum + jnp.sum(pieces[j].astype(jnp.float32), axis=0, keepdims=True)
-    grad_bias[...] = bias_sum
     for copy in last:
         copy.wait_recv()
     for copy, when in pending:
@@ -402,20 +392,19 @@
         (PARTS + 6) * (groups - 1) + PARTS * (4 * chips - 3) + 3 * chips - 2 + shards_of - 1
     )
     vmem = pl.BlockSpec(memory_space=pltpu.VMEM)
-    hidden, grad_weight, grad_bias, back, gain_sums = pl.pallas_call(
+    hidden, columns, pieces, back, gain_sums = pl.pallas_call(
         functools.partial(fused_kernel, groups, shards_of),
         out_shape=[
             jax.ShapeDtypeStruct((rows, hidden_units), bf16),
-            jax.ShapeDtypeStruct((2 * width, hidden_units), bf16),
-            jax.ShapeDtypeStruct((1, hidden_units), f32),
+            jax.ShapeDtypeStruct((groups, rows, 2 * width), bf16),
+            jax.ShapeDtypeStruct((groups, rows, hidden_units), bf16),
             jax.ShapeDtypeStruct((groups, rows, width), bf16),
             jax.ShapeDtypeStruct((groups, 8, width), f32),
         ],
-        in_specs=[vmem] * 4 + [pl.BlockSpec(memory_space=pl.ANY)],
+        in_specs=[vmem] * 3 + [pl.BlockSpec(memory_space=pl.ANY)] * 2,
         out_specs=[vmem] * 5,
         scratch_shapes=[
-            pltpu.VMEM((groups, rows, 2 * width), bf16),
-            pltpu.VMEM((groups, rows, hidden_units), bf16),
+            pltpu.VMEM((rows, hidden_units), bf16),
             pltpu.VMEM(w_up.shape, bf16),
             pltpu.VMEM((groups - 1, rows, width), bf16),
             pltpu.VMEM((shards_of, rows, width), bf16),
@@ -431,6 +420,7 @@
             pltpu.SemaphoreType.DMA((copies,)),
             pltpu.SemaphoreType.DMA((copies,)),
             pltpu.SemaphoreType.DMA,
+            pltpu.SemaphoreType.DMA,
         ],
         compiler_params=pltpu.CompilerParams(
             collective_id=0, has_side_effects=True, vmem_limit_bytes=50 * 1024 * 1024
@@ -438,8 +428,9 @@
     )(outgoing, gain.reshape(shards_of, 1, width), bias[None], grad_hidden, w_up)
     return (
         hidden,
-        grad_weight,
-        grad_bias[0],
+        *weight_gradients(
+            columns.reshape(groups * rows, 2 * width), pieces.reshape(groups * rows, hidden_units)
+        ),
         back.reshape(groups * rows, width),
         jnp.sum(gain_sums[:, 0], axis=0),
     )

time: 84.7 us -> 82.6 us (0.975)
  local copies, waits for them, and re-layouts: 8.93 us -> 3.13 us
  matrix products: 1.89 us -> 6.15 us
    unnamed x8 -> x9, local copies, waits for them, and re-layouts: 7.31 us -> 1.5 us
    dot_general x0 -> x1, matrix products: none -> 4.27 us  [weight_gradients(): lax.dot_general(column_rows, piece, (((0,), (0,)), ((), ())), preferred_e...]
    reduce_sum x0 -> x1, other arithmetic: none -> 0.86 us  [weight_gradients(): return (grad_weight, jnp.sum(piece.astype(jnp.float32), axis=0))]
where the time goes in v5:
time: 82.6 us; the launch traced here: 82.4 us
  Pallas kernels  69.9 us (85%)
  matrix products  6.15 us (7%)
  local copies, waits for them, and re-layouts  3.13 us (4%)
  other arithmetic  2.5 us (3%)
    pallas_call x1, Pallas kernels, fused(): pl.pallas_call(functools.partial(fused_kernel, groups, shards_of), out_sh...  69.9 us
    dot_general x1, matrix products, weight_gradients(): lax.dot_general(column_rows, piece, (((0,), (0,)), ((), ())), preferred_e...  4.27 us

profile of v5, /device:TPU:0, one launch (start us, length us, event | category | flops | bytes accessed | tf_op | source)
XLA Modules:
  0.0 82.4 jit_solution(15210106564544451000)
XLA Ops:
  0.6 0.0 copy-start
  0.6 0.0 copy-start.1
  0.7 0.8 %broadcast_in_dim.32 = s32[32]{0:T(128)S(1)} reshape(s32[4,8]{1,0:T(4,128)} %param.12) | data formatting | bytes 256 | tf_op jit(solution)/shard_map/jit(_where)/broadcast_in_dim | solution.py:30
  1.5 0.7 and_select_fusion.1
  2.2 0.2 select_reduce_fusion.1
  2.5 0.1 add_select_fusion
  2.5 0.1 select_n.46
  2.6 0.7 broadcast_in_dim.36.bias
  3.3 0.0 copy-done
  3.3 0.6 convolution_convert_fusion
  3.9 0.0 copy-done.1
  3.9 0.0 copy-start.2
  3.9 0.7 copy-done.2
  4.7 69.9 %shard_map.110 = (bf16[128,1536]{1,0:T(8,128)(2,1)S(1)}, bf16[4,128,1536]{2,1,0:T(8,128)(2,1)S(1)}, bf16[4,128,1536]{2,1,0:T(8,128)(2,1)}, bf16[4,128,768]{2,1,0:T(8,128)(2,1)S(1)}, f32[4,8,768]{2,1,0:T(8,128)S(1)}) custom-call(bf16[4,128,768]{2,1,0:T(8,128)(2,1)S(1)} %bitcast.9, f32[8,1,768]{2,1,0:T(1,128)S(1)} %bitcast.10, ...), custom_call_target="tpu_custom_call" | custom-call | tf_op jit(solution)/shard_map/pallas_call | solution.py:395
  74.6 0.0 copy-start.3
  74.6 1.3 %convolution_convert_fusion.1 = bf16[384,768]{1,0:T(8,128)(2,1)} fusion(bf16[512,768]{1,0:T(8,128)(2,1)S(1)} %bitcast.11, s32[384]{0:T(512)S(1)} %select_n.46), kind=kOutput, calls=%fused_computation.3 | convolution fusion | flops 302481408 | bytes 1377792 | tf_op jit(solution)/shard_map/dot_general | solution.py:464
  75.9 0.6 slice_reduce_fusion
  76.5 0.0 copy-done.3
  76.5 0.9 %convert_reduce_fusion = f32[1536]{0:T(1024)} fusion(bf16[4,128,1536]{2,1,0:T(8,128)(2,1)S(1)} %copy-done.3), kind=kLoop, calls=%fused_computation.1 | loop fusion | flops 1571328 | bytes 1579008 | tf_op jit(solution)/shard_map/reduce_sum | solution.py:47
  77.4 4.3 %bitcast_convert_fusion = bf16[1536,1536]{1,0:T(8,128)(2,1)} fusion(bf16[4,128,1536]{2,1,0:T(8,128)(2,1)S(1)} %get-tuple-element.12, bf16[4,128,1536]{2,1,0:T(8,128)(2,1)S(1)} %copy-done.3), kind=kOutput, calls=%fused_computation | convolution fusion | flops 2418278400 | bytes 7864320 | tf_op jit(solution)/shard_map/dot_general | solution.py:44
  81.6 0.7 copy.16
  (2 shorter events, 0.0 us)
Async XLA Ops:
  0.6 2.7 %copy-start = (bf16[384,768]{1,0:T(8,128)(2,1)S(1)}, bf16[384,768]{1,0:T(8,128)(2,1)}, u32[]{:S(2)}) copy-start(bf16[384,768]{1,0:T(8,128)(2,1)} %param.7) | copy-start | bytes 1769476
  0.6 3.3 %copy-start.1 = (bf16[128,1536]{1,0:T(8,128)(2,1)S(1)}, bf16[128,1536]{1,0:T(8,128)(2,1)}, u32[]{:S(2)}) copy-start(bf16[128,1536]{1,0:T(8,128)(2,1)} %grad_hidden_hbm.1) | copy-start | bytes 1179652
  3.9 0.7 copy-start.2
  74.6 2.0 %copy-start.3 = (bf16[4,128,1536]{2,1,0:T(8,128)(2,1)S(1)}, bf16[4,128,1536]{2,1,0:T(8,128)(2,1)}, u32[]{:S(2)}) copy-start(bf16[4,128,1536]{2,1,0:T(8,128)(2,1)} %get-tuple-element.13) | copy-start | bytes 4718596
